TPU v7x, 32 devices: a whole 2x2x4 slice. The times are simulated.
32 devices in a mesh: dp: 4 (over y, core), space: 8 (over z, x).
Axes of the slice: x: 2, y: 2, z: 4, core: 2. Of those that a mesh axis runs over, the one named last changes fastest.
Arguments:
- fields: bfloat16 [4, 8, 2, 16, 64, 128], P('dp', 'space'), may hold values from -6 to 6
- conv_fine: bfloat16 [27, 128, 128], replicated, may hold values from -0.109375 to 0.109375
- conv_down: bfloat16 [1024, 256], replicated, may hold values from -0.1875 to 0.1875
- conv_depth: float32 [27, 256], replicated, may hold values from -1.5 to 1.5
- norm_gain: float32 [256], replicated, may hold values from 0.5 to 2
- conv_point: bfloat16 [256, 256], replicated, may hold values from -0.375 to 0.375
- upstream: bfloat16 [4, 8, 1, 8, 32, 256], P('dp', 'space'), may hold values from -6 to 6
Outputs:
- coarse_out: bfloat16 [4, 8, 1, 8, 32, 256], P('dp', 'space')
- grad_fine: float32 [27, 128, 128], replicated
- grad_down: float32 [1024, 256], replicated
- grad_depth_w: float32 [27, 256], replicated
- grad_gain: float32 [256], replicated
- grad_point: float32 [256, 256], replicated
All inputs are finite; a program needn't handle non-finite values.
Results may differ from a plain program's by a relative error of at most 0.0081.
Values may be sent and summed in bfloat16 or wider, within the bound.
A program may use at most 128 MiB of HBM per device.

v0:
```python
import jax
import jax.numpy as jnp
from jax import lax
from jax.sharding import PartitionSpec as P

eps = 1e-05


def shifted(block, axis, distance):
    devices = range(lax.axis_size(axis))
    route = [((i - distance) % len(devices), i) for i in devices]
    return lax.ppermute(block, axis, route)


def shifted_2(value, axis, by):
    count = lax.axis_size(axis)
    pairs = [(i, i + by) for i in range(count) if 0 <= i + by < count]
    return lax.ppermute(value, axis, pairs)


def tap_offsets(tap_index):
    return (tap_index // 9, tap_index // 3 % 3, tap_index % 3)


def pad_sides(field, which_dims):
    widths = [(0, 0)] * field.ndim
    for dim_index in which_dims:
        widths[dim_index] = (1, 1)
    return jnp.pad(field, widths)


def full_conv(padded, w_taps):
    ext_x, ext_y, ext_z = (padded.shape[0] - 2, padded.shape[1] - 2, padded.shape[2] - 2)
    summed = jnp.zeros((ext_x * ext_y * ext_z, w_taps.shape[2]), jnp.float32)
    for tap_index in range(27):
        shift_x, shift_y, shift_z = tap_offsets(tap_index)
        window = padded[
            shift_x : shift_x + ext_x, shift_y : shift_y + ext_y, shift_z : shift_z + ext_z
        ].reshape(-1, padded.shape[3])
        summed = summed + jnp.dot(window, w_taps[tap_index], preferred_element_type=jnp.float32)
    return summed


def tap_grads(padded, grad_rows):
    ext_x, ext_y, ext_z = (padded.shape[0] - 2, padded.shape[1] - 2, padded.shape[2] - 2)
    result = []
    for tap_index in range(27):
        shift_x, shift_y, shift_z = tap_offsets(tap_index)
        window = padded[
            shift_x : shift_x + ext_x, shift_y : shift_y + ext_y, shift_z : shift_z + ext_z
        ].reshape(-1, padded.shape[3])
        result.append(
            lax.dot_general(
                window, grad_rows, (((0,), (0,)), ((), ())), preferred_element_type=jnp.float32
            )
        )
    return jnp.stack(result)


def depth_conv(padded, weights):
    ext_x, ext_y, ext_z = (padded.shape[0] - 2, padded.shape[1] - 2, padded.shape[2] - 2)
    summed = jnp.zeros((ext_x, ext_y, ext_z, padded.shape[3]), jnp.float32)
    for tap_index in range(27):
        shift_x, shift_y, shift_z = tap_offsets(tap_index)
        window = padded[
            shift_x : shift_x + ext_x, shift_y : shift_y + ext_y, shift_z : shift_z + ext_z
        ]
        summed = summed + window.astype(jnp.float32) * weights[tap_index]
    return summed


def depth_taps(padded, grad_field):
    ext_x, ext_y, ext_z = (padded.shape[0] - 2, padded.shape[1] - 2, padded.shape[2] - 2)
    grad_f = grad_field.astype(jnp.float32)
    result = []
    for tap_index in range(27):
        shift_x, shift_y, shift_z = tap_offsets(tap_index)
        window = padded[
            shift_x : shift_x + ext_x, shift_y : shift_y + ext_y, shift_z : shift_z + ext_z
        ]
        result.append(jnp.sum(window.astype(jnp.float32) * grad_f, axis=(0, 1, 2)))
    return jnp.stack(result)


def to_blocks(grid):
    ext_x, ext_y, ext_z, chans = grid.shape
    split = grid.reshape(ext_x // 2, 2, ext_y // 2, 2, ext_z // 2, 2, chans)
    return split.transpose(0, 2, 4, 1, 3, 5, 6).reshape(-1, 8 * chans)


def from_blocks(rows, ext_x, ext_y, ext_z, chans):
    split = rows.reshape(ext_x // 2, ext_y // 2, ext_z // 2, 2, 2, 2, chans)
    return split.transpose(0, 3, 1, 4, 2, 5, 6).reshape(-1, chans)


def silu_slope(value):
    sigma = jax.nn.sigmoid(value)
    return sigma * (1.0 + value * (1.0 - sigma))


def quarter_totals(vector, slices):
    total = vector
    for stride in (slices, 2 * slices):
        total = total + shifted(total, "space", stride)
    return total


def fine_halo(fine):
    row_pos = lax.axis_index("space") % 4
    pieces = []
    for step, edge, fence in ((1, fine[:, -1:], 0), (-1, fine[:, :1], 3)):
        got = shifted_2(edge, "space", step)
        pieces.append(jnp.where(row_pos == fence, jnp.zeros_like(got), got))
    wide = jnp.concatenate([pieces[0], fine, pieces[1]], axis=1)
    sides = []
    for step, edge in ((4, wide[-1:]), (-4, wide[:1])):
        sides.append(shifted_2(edge, "space", step))
    return jnp.concatenate([sides[0], wide, sides[1]], axis=0)


def local(fields, conv_fine, conv_down, conv_depth, norm_gain, conv_point, upstream):
    nodes = lax.axis_size("space")
    slices = nodes // 4
    fine = fields[0, 0]
    brick_x, brick_y, brick_z, chan_fine = fine.shape
    fine_pad = pad_sides(fine_halo(fine), (2,))
    pre_act = full_conv(fine_pad, conv_fine)
    act = jax.nn.silu(pre_act).astype(jnp.bfloat16)
    blocks = to_blocks(act.reshape(brick_x, brick_y, brick_z, chan_fine))
    coarse = jnp.dot(blocks, conv_down, preferred_element_type=jnp.float32).astype(jnp.bfloat16)
    chan_coarse = coarse.shape[1]
    cell_x = brick_x // 2
    cell_y = brick_y // 2
    cell_z = brick_z // 2
    coarse_brick = coarse.reshape(cell_x, cell_y, cell_z, chan_coarse)
    count = nodes // 4 * cell_x * 4 * cell_y * cell_z
    part_width = chan_coarse // slices
    quarter = cell_z // 4
    offset = lax.axis_index("space") % slices * part_width
    depth_w = lax.dynamic_slice_in_dim(conv_depth, offset, part_width, 1)
    gain_w = lax.dynamic_slice_in_dim(norm_gain, offset, part_width, 0)

    def pad_local(field):
        below = shifted_2(field[:, :, -1:], "space", slices)
        above = shifted_2(field[:, :, :1], "space", -slices)
        return pad_sides(jnp.concatenate([below, field, above], axis=2), (0, 1))

    def stat_totals(vector):
        return quarter_totals(vector, slices)

    def place_vec(vector):
        zeros_full = jnp.zeros(vector.shape[:-1] + (chan_coarse,), jnp.float32)
        return lax.dynamic_update_slice_in_dim(zeros_full, vector, offset, vector.ndim - 1)

    def to_local(field):
        parts = field.reshape(cell_x, cell_y, 4, quarter, slices, part_width)
        parts = parts.transpose(2, 4, 0, 1, 3, 5).reshape(
            nodes, cell_x, cell_y, quarter, part_width
        )
        got = lax.all_to_all(parts, "space", split_axis=0, concat_axis=0, tiled=True)
        got = got.reshape(nodes // 4, 4, cell_x, cell_y, quarter, part_width)
        return got.transpose(0, 2, 1, 3, 4, 5).reshape(
            nodes // 4 * cell_x, 4 * cell_y, quarter, part_width
        )

    def to_brick(field):
        parts = field.reshape(nodes // 4, cell_x, 4, cell_y, quarter, part_width)
        parts = parts.transpose(0, 2, 1, 3, 4, 5).reshape(
            nodes, cell_x, cell_y, quarter, part_width
        )
        got = lax.all_to_all(parts, "space", split_axis=0, concat_axis=0, tiled=True)
        got = got.reshape(4, slices, cell_x, cell_y, quarter, part_width)
        return got.transpose(2, 3, 0, 4, 1, 5).reshape(cell_x, cell_y, cell_z, chan_coarse)

    local_grid = to_local(coarse_brick)
    local_pad = pad_local(local_grid)
    depth_out = depth_conv(local_pad, depth_w)
    square_sum = stat_totals(jnp.sum(depth_out * depth_out, axis=(0, 1, 2)))
    scale = lax.rsqrt(square_sum / count + eps)
    normed = (depth_out * (gain_w * scale)).astype(jnp.bfloat16)
    normed_rows = to_brick(normed).reshape(-1, chan_coarse)
    activated = jax.nn.silu(normed_rows.astype(jnp.float32)).astype(jnp.bfloat16)
    outcome = coarse.astype(jnp.float32) + jnp.dot(
        activated, conv_point, preferred_element_type=jnp.float32
    )
    coarse_out = outcome.astype(jnp.bfloat16).reshape(1, 1, cell_x, cell_y, cell_z, chan_coarse)
    grad_rows = upstream.reshape(-1, chan_coarse)
    grad_point = lax.dot_general(
        activated, grad_rows, (((0,), (0,)), ((), ())), preferred_element_type=jnp.float32
    )
    grad_act = lax.dot_general(
        grad_rows, conv_point, (((1,), (1,)), ((), ())), preferred_element_type=jnp.float32
    )
    grad_normed = (grad_act * silu_slope(normed_rows.astype(jnp.float32))).astype(jnp.bfloat16)
    grad_f = to_local(grad_normed.reshape(cell_x, cell_y, cell_z, chan_coarse)).astype(jnp.float32)
    cross_local = jnp.sum(grad_f * depth_out, axis=(0, 1, 2))
    cross = stat_totals(cross_local)
    gain_part = place_vec(scale * cross_local)
    grad_depth_in = (
        gain_w * scale * grad_f - depth_out * (gain_w * scale * scale * scale / count) * cross
    ).astype(jnp.bfloat16)
    depth_part = place_vec(depth_taps(local_pad, grad_depth_in))
    back_depth = depth_conv(pad_local(grad_depth_in), depth_w[::-1]).astype(jnp.bfloat16)
    back_rows = to_brick(back_depth).reshape(-1, chan_coarse)
    grad_coarse = (grad_rows.astype(jnp.float32) + back_rows.astype(jnp.float32)).astype(
        jnp.bfloat16
    )
    grad_down = lax.dot_general(
        blocks, grad_coarse, (((0,), (0,)), ((), ())), preferred_element_type=jnp.float32
    )
    grad_blocks = lax.dot_general(
        grad_coarse, conv_down, (((1,), (1,)), ((), ())), preferred_element_type=jnp.float32
    )
    grad_act_fine = from_blocks(grad_blocks, brick_x, brick_y, brick_z, chan_fine)
    grad_pre = (grad_act_fine * silu_slope(pre_act)).astype(jnp.bfloat16)
    grad_fine = tap_grads(fine_pad, grad_pre)
    totals = lax.psum((grad_fine, grad_down, depth_part, gain_part, grad_point), ("dp", "space"))
    return (coarse_out, totals[0], totals[1], totals[2], totals[3], totals[4])


def solution(mesh):
    placed = (
        P("dp", "space", None, None, None, None),
        P(),
        P(),
        P(),
        P(),
        P(),
        P("dp", "space", None, None, None, None),
    )
    return jax.shard_map(
        local,
        mesh=mesh,
        in_specs=placed,
        out_specs=(P("dp", "space", None, None, None, None), P(), P(), P(), P(), P()),
        check_vma=False,
    )
```

profile of v0, /device:TPU:0, one launch (start us, length us, event | category | flops | bytes accessed | tf_op | source)
XLA Modules:
  0.0 303.7 jit_solution(17436524571360375886)
XLA Ops:
  8.1 4.8 %collective-permute-start = (bf16[2,1,64,128]{3,2,1,0:T(8,128)(2,1)S(1)}, bf16[2,1,64,128]{3,2,1,0:T(8,128)(2,1)S(1)}, u32[]{:S(2)}, u32[]{:S(2)}) collective-permute-start(bf16[2,1,64,128]{3,2,1,0:T(8,128)(2,1)S(1)} %get-tuple-element.76), channel_id=1, source_target_pairs={{0,1},{1,2},{2,3},{3,4},{4,5},{5,6},{6,7},{8,9},{9,10},{10,11},{11... | collective-permute-start | bytes 98312 | tf_op jit(solution)/shard_map/ppermute | solution.py:18
  12.9 1.3 collective-permute-start.1
  14.5 4.2 %collective-permute-done.1 = bf16[2,1,64,128]{3,2,1,0:T(8,128)(2,1)S(1)} collective-permute-done((bf16[2,1,64,128]{3,2,1,0:T(8,128)(2,1)S(1)}, bf16[2,1,64,128]{3,2,1,0:T(8,128)(2,1)S(1)}, u32[]{:S(2)}, u32[]{:S(2)}) %collective-permute-start.1) | collective-permute-done | bytes 32800 | tf_op jit(solution)/shard_map/ppermute | solution.py:18
  19.9 4.5 %collective-permute-start.2 = (bf16[1,18,64,128]{3,2,1,0:T(8,128)(2,1)S(1)}, bf16[1,18,64,128]{3,2,1,0:T(8,128)(2,1)S(1)}, u32[]{:S(2)}, u32[]{:S(2)}) collective-permute-start(bf16[1,18,64,128]{3,2,1,0:T(8,128)(2,1)S(1)} %get-tuple-element.72), channel_id=1, source_target_pairs={{0,4},{1,5},{2,6},{3,7},{8,12},{9,13},{10,14},{11,15},{16,20},{17,... | collective-permute-start | bytes 884744 | tf_op jit(solution)/shard_map/ppermute | solution.py:18
  24.4 1.3 collective-permute-start.3
  25.8 3.4 %collective-permute-done.2 = bf16[1,18,64,128]{3,2,1,0:T(8,128)(2,1)S(1)} collective-permute-done((bf16[1,18,64,128]{3,2,1,0:T(8,128)(2,1)S(1)}, bf16[1,18,64,128]{3,2,1,0:T(8,128)(2,1)S(1)}, u32[]{:S(2)}, u32[]{:S(2)}) %collective-permute-start.2) | collective-permute-done | bytes 294944 | tf_op jit(solution)/shard_map/ppermute | solution.py:18
  29.3 11.3 %collective-permute-done.3 = bf16[1,18,64,128]{3,2,1,0:T(8,128)(2,1)S(1)} collective-permute-done((bf16[1,18,64,128]{3,2,1,0:T(8,128)(2,1)S(1)}, bf16[1,18,64,128]{3,2,1,0:T(8,128)(2,1)S(1)}, u32[]{:S(2)}, u32[]{:S(2)}) %collective-permute-start.3) | collective-permute-done | bytes 294944 | tf_op jit(solution)/shard_map/ppermute | solution.py:18
  41.2 2.6 fusion.176
  53.8 1.3 multiply_convert_fusion.1
  56.3 1.4 reshape.261
  58.8 3.4 %all-to-all-start = ((bf16[8,1,8,8,128]{4,3,2,1,0:T(8,128)(2,1)}), bf16[8,1,8,8,128]{4,3,2,1,0:T(8,128)(2,1)S(1)}, u32[]{:S(2)}, u32[]{:S(2)}) async-start(bf16[8,1,8,8,128]{4,3,2,1,0:T(8,128)(2,1)} %bitcast.59), calls=%async_computation | async-start | bytes 262144 | tf_op jit(solution)/shard_map/all_to_all | solution.py:160
  63.4 6.0 %all-to-all-done = bf16[8,1,8,8,128]{4,3,2,1,0:T(8,128)(2,1)S(1)} async-done(((bf16[8,1,8,8,128]{4,3,2,1,0:T(8,128)(2,1)}), bf16[8,1,8,8,128]{4,3,2,1,0:T(8,128)(2,1)S(1)}, u32[]{:S(2)}, u32[]{:S(2)}) %all-to-all-start) | async-done | bytes 131104 | tf_op jit(solution)/shard_map/all_to_all | solution.py:160
  69.5 1.8 collective-permute-start.4
  71.2 1.3 collective-permute-start.5
  73.6 3.4 %collective-permute-done.5 = bf16[2,32,1,128]{3,2,1,0:T(2,128)(2,1)S(1)} collective-permute-done((bf16[2,32,1,128]{3,2,1,0:T(2,128)(2,1)S(1)}, bf16[2,32,1,128]{3,2,1,0:T(2,128)(2,1)S(1)}, u32[]{:S(2)}, u32[]{:S(2)}) %collective-permute-start.5) | collective-permute-done | bytes 16416 | tf_op jit(solution)/shard_map/ppermute | solution.py:18
  79.4 4.2 %collective-permute-done.6 = f32[128]{0:T(128)S(1)} collective-permute-done((f32[128]{0:T(128)S(1)}, f32[128]{0:T(128)S(1)}, u32[]{:S(2)}, u32[]{:S(2)}) %collective-permute-start.6) | collective-permute-done | bytes 544 | tf_op jit(solution)/shard_map/ppermute | solution.py:12
  83.6 4.4 %collective-permute-done.7 = f32[128]{0:T(128)S(1)} collective-permute-done((f32[128]{0:T(128)S(1)}, f32[128]{0:T(128)S(1)}, u32[]{:S(2)}, u32[]{:S(2)}) %collective-permute-start.7) | collective-permute-done | bytes 544 | tf_op jit(solution)/shard_map/ppermute | solution.py:12
  88.2 10.0 %all_to_all.20 = bf16[8,1,8,8,128]{4,3,2,1,0:T(8,128)(2,1)S(1)} all-to-all(bf16[8,1,8,8,128]{4,3,2,1,0:T(8,128)(2,1)S(1)} %bitcast.538), channel_id=1, replica_groups=mesh['dp'=4,'space'=8] {'space'}, dimensions={0} | all-to-all | bytes 262144 | tf_op jit(solution)/shard_map/all_to_all | solution.py:171
  99.0 9.7 %all_to_all.21 = bf16[8,1,8,8,128]{4,3,2,1,0:T(8,128)(2,1)S(1)} all-to-all(bf16[8,1,8,8,128]{4,3,2,1,0:T(8,128)(2,1)S(1)} %bitcast.537), channel_id=1, replica_groups=mesh['dp'=4,'space'=8] {'space'}, dimensions={0} | all-to-all | bytes 262144 | tf_op jit(solution)/shard_map/all_to_all | solution.py:160
  108.8 5.3 %collective-permute-done.8 = f32[128]{0:T(128)S(1)} collective-permute-done((f32[128]{0:T(128)S(1)}, f32[128]{0:T(128)S(1)}, u32[]{:S(2)}, u32[]{:S(2)}) %collective-permute-start.8) | collective-permute-done | bytes 544 | tf_op jit(solution)/shard_map/ppermute | solution.py:12
  114.3 4.4 %collective-permute-done.9 = f32[128]{0:T(128)S(1)} collective-permute-done((f32[128]{0:T(128)S(1)}, f32[128]{0:T(128)S(1)}, u32[]{:S(2)}, u32[]{:S(2)}) %collective-permute-start.9) | collective-permute-done | bytes 544 | tf_op jit(solution)/shard_map/ppermute | solution.py:12
  120.1 1.3 collective-permute-start.10
  121.4 1.3 collective-permute-start.11
  123.4 3.8 %collective-permute-done.11 = bf16[2,32,1,128]{3,2,1,0:T(2,128)(2,1)S(1)} collective-permute-done((bf16[2,32,1,128]{3,2,1,0:T(2,128)(2,1)S(1)}, bf16[2,32,1,128]{3,2,1,0:T(2,128)(2,1)S(1)}, u32[]{:S(2)}, u32[]{:S(2)}) %collective-permute-start.11) | collective-permute-done | bytes 16416 | tf_op jit(solution)/shard_map/ppermute | solution.py:18
  127.4 1.6 fusion.114
  129.0 4.0 %all-to-all-start.3 = ((bf16[8,1,8,8,128]{4,3,2,1,0:T(8,128)(2,1)}), bf16[8,1,8,8,128]{4,3,2,1,0:T(8,128)(2,1)}, u32[]{:S(2)}, u32[]{:S(2)}) async-start(bf16[8,1,8,8,128]{4,3,2,1,0:T(8,128)(2,1)} %bitcast.533), calls=%async_computation.3 | async-start | bytes 262144 | tf_op jit(solution)/shard_map/all_to_all | solution.py:171
  133.0 1.9 fusion.184
  134.9 5.4 %all-to-all-done.3 = bf16[8,1,8,8,128]{4,3,2,1,0:T(8,128)(2,1)} async-done(((bf16[8,1,8,8,128]{4,3,2,1,0:T(8,128)(2,1)}), bf16[8,1,8,8,128]{4,3,2,1,0:T(8,128)(2,1)}, u32[]{:S(2)}, u32[]{:S(2)}) %all-to-all-start.3) | async-done | bytes 131104 | tf_op jit(solution)/shard_map/all_to_all | solution.py:171
  154.4 1.3 fusion.183
  158.5 39.6 %all-reduce.3 = (f32[27,256]{1,0:T(8,128)}, f32[256]{0:T(256)}) all-reduce(f32[27,256]{1,0:T(8,128)S(1)} %constant_dynamic-update-slice_fusion, f32[256]{0:T(256)S(1)} %copy-done.91), channel_id=1, replica_groups=mesh['dp'=4,'space'=8] {'dp','space'}, use_global_device_ids=true, to_apply=%region_31.32 | all-reduce | flops 7168 | bytes 57344 | tf_op jit(solution)/shard_map/psum | solution.py:217
  198.1 94.0 %all-reduce.7.cloned.1.call-done = (f32[27,128,128]{2,1,0:T(8,128)}, f32[1024,256]{1,0:T(8,128)}, f32[256,256]{1,0:T(8,128)}) async-done(((f32[27,128,128]{2,1,0:T(8,128)}, f32[1024,256]{1,0:T(8,128)}, f32[256,256]{1,0:T(8,128)}), (f32[27,128,128]{2,1,0:T(8,128)}, f32[1024,256]{1,0:T(8,128)}, f32[256,256]{1,0:T(8,128)})) %all-reduce.7.cloned.1.call-update) | async-done | bytes 3080208 | tf_op jit(solution)/shard_map/psum | solution.py:217
  292.1 3.0 copy.69
  (294 shorter events, 40.6 us)
Async XLA Ops:
  7.2 50.6 %copy-start = (bf16[1024,256]{1,0:T(8,128)(2,1)S(1)}, bf16[1024,256]{1,0:T(8,128)(2,1)}, u32[]{:S(2)}) copy-start(bf16[1024,256]{1,0:T(8,128)(2,1)} %param.9) | copy-start | bytes 1572868
  7.2 18.5 %copy-start.1 = (bf16[1,1,2,16,64,128]{5,4,3,2,1,0:T(8,128)(2,1)S(1)}, bf16[1,1,2,16,64,128]{5,4,3,2,1,0:T(8,128)(2,1)}, u32[]{:S(2)}) copy-start(bf16[1,1,2,16,64,128]{5,4,3,2,1,0:T(8,128)(2,1)} %param.7) | copy-start | bytes 1572868
  8.1 6.4 %collective-permute-start = (bf16[2,1,64,128]{3,2,1,0:T(8,128)(2,1)S(1)}, bf16[2,1,64,128]{3,2,1,0:T(8,128)(2,1)S(1)}, u32[]{:S(2)}, u32[]{:S(2)}) collective-permute-start(bf16[2,1,64,128]{3,2,1,0:T(8,128)(2,1)S(1)} %get-tuple-element.76), channel_id=1, source_target_pairs={{0,1},{1,2},{2,3},{3,4},{4,5},{5,6},{6,7},{8,9},{9,10},{10,11},{11... | collective-permute-start | bytes 98312 | tf_op jit(solution)/shard_map/ppermute | solution.py:18
  12.9 5.8 %collective-permute-start.1 = (bf16[2,1,64,128]{3,2,1,0:T(8,128)(2,1)S(1)}, bf16[2,1,64,128]{3,2,1,0:T(8,128)(2,1)S(1)}, u32[]{:S(2)}, u32[]{:S(2)}) collective-permute-start(bf16[2,1,64,128]{3,2,1,0:T(8,128)(2,1)S(1)} %get-tuple-element.77), channel_id=1, source_target_pairs={{1,0},{2,1},{3,2},{4,3},{5,4},{6,5},{7,6},{9,8},{10,9},{11,10},{12... | collective-permute-start | bytes 98312 | tf_op jit(solution)/shard_map/ppermute | solution.py:18
  19.9 9.4 %collective-permute-start.2 = (bf16[1,18,64,128]{3,2,1,0:T(8,128)(2,1)S(1)}, bf16[1,18,64,128]{3,2,1,0:T(8,128)(2,1)S(1)}, u32[]{:S(2)}, u32[]{:S(2)}) collective-permute-start(bf16[1,18,64,128]{3,2,1,0:T(8,128)(2,1)S(1)} %get-tuple-element.72), channel_id=1, source_target_pairs={{0,4},{1,5},{2,6},{3,7},{8,12},{9,13},{10,14},{11,15},{16,20},{17,... | collective-permute-start | bytes 884744 | tf_op jit(solution)/shard_map/ppermute | solution.py:18
  24.4 16.2 %collective-permute-start.3 = (bf16[1,18,64,128]{3,2,1,0:T(8,128)(2,1)S(1)}, bf16[1,18,64,128]{3,2,1,0:T(8,128)(2,1)S(1)}, u32[]{:S(2)}, u32[]{:S(2)}) collective-permute-start(bf16[1,18,64,128]{3,2,1,0:T(8,128)(2,1)S(1)} %get-tuple-element.73), channel_id=1, source_target_pairs={{4,0},{5,1},{6,2},{7,3},{12,8},{13,9},{14,10},{15,11},{20,16},{21,... | collective-permute-start | bytes 884744 | tf_op jit(solution)/shard_map/ppermute | solution.py:18
  25.8 23.3 %copy-start.8 = (bf16[2,16,64,128]{3,2,1,0:T(8,128)(2,1)}, bf16[2,16,64,128]{3,2,1,0:T(8,128)(2,1)S(1)}, u32[]{:S(2)}) copy-start(bf16[2,16,64,128]{3,2,1,0:T(8,128)(2,1)S(1)} %get-tuple-element.75) | copy-start | bytes 1572868
  44.0 8.9 %copy-start.2 = (bf16[2,16,64,128]{3,2,1,0:T(8,128)(2,1)}, bf16[2,16,64,128]{3,2,1,0:T(8,128)(2,1)S(1)}, u32[]{:S(2)}) copy-start(bf16[2,16,64,128]{3,2,1,0:T(8,128)(2,1)S(1)} %get-tuple-element.48) | copy-start | bytes 1572868
  44.0 9.8 %copy-start.48 = (bf16[2,16,64,128]{3,2,1,0:T(8,128)(2,1)}, bf16[2,16,64,128]{3,2,1,0:T(8,128)(2,1)S(1)}, u32[]{:S(2)}) copy-start(bf16[2,16,64,128]{3,2,1,0:T(8,128)(2,1)S(1)} %get-tuple-element.46) | copy-start | bytes 1572868
  57.7 15.9 %copy-start.42 = (bf16[256,1024]{1,0:T(8,128)(2,1)}, bf16[256,1024]{1,0:T(8,128)(2,1)S(1)}, u32[]{:S(2)}) copy-start(bf16[256,1024]{1,0:T(8,128)(2,1)S(1)} %reshape.261) | copy-start | bytes 1572868
  58.8 10.7 %all-to-all-start = ((bf16[8,1,8,8,128]{4,3,2,1,0:T(8,128)(2,1)}), bf16[8,1,8,8,128]{4,3,2,1,0:T(8,128)(2,1)S(1)}, u32[]{:S(2)}, u32[]{:S(2)}) async-start(bf16[8,1,8,8,128]{4,3,2,1,0:T(8,128)(2,1)} %bitcast.59), calls=%async_computation | async-start | bytes 262144 | tf_op jit(solution)/shard_map/all_to_all | solution.py:160
  63.3 14.9 %copy-start.60 = (f32[128]{0:T(128)}, f32[128]{0:T(128)S(1)}, u32[]{:S(2)}) copy-start(f32[128]{0:T(128)S(1)} %get-tuple-element.94) | copy-start | bytes 1540
  63.3 14.9 %copy-start.62 = (f32[128]{0:T(128)}, f32[128]{0:T(128)S(1)}, u32[]{:S(2)}) copy-start(f32[128]{0:T(128)S(1)} %get-tuple-element.95) | copy-start | bytes 1540
  63.3 14.9 %copy-start.64 = (f32[128]{0:T(128)}, f32[128]{0:T(128)S(1)}, u32[]{:S(2)}) copy-start(f32[128]{0:T(128)S(1)} %get-tuple-element.96) | copy-start | bytes 1540
  63.3 14.9 %copy-start.66 = (f32[128]{0:T(128)}, f32[128]{0:T(128)S(1)}, u32[]{:S(2)}) copy-start(f32[128]{0:T(128)S(1)} %get-tuple-element.97) | copy-start | bytes 1540
  63.4 14.9 %copy-start.68 = (f32[128]{0:T(128)}, f32[128]{0:T(128)S(1)}, u32[]{:S(2)}) copy-start(f32[128]{0:T(128)S(1)} %get-tuple-element.98) | copy-start | bytes 1540
  63.4 14.9 %copy-start.70 = (f32[128]{0:T(128)}, f32[128]{0:T(128)S(1)}, u32[]{:S(2)}) copy-start(f32[128]{0:T(128)S(1)} %get-tuple-element.99) | copy-start | bytes 1540
  69.5 4.1 %collective-permute-start.4 = (bf16[2,32,1,128]{3,2,1,0:T(2,128)(2,1)S(1)}, bf16[2,32,1,128]{3,2,1,0:T(2,128)(2,1)S(1)}, u32[]{:S(2)}, u32[]{:S(2)}) collective-permute-start(bf16[2,32,1,128]{3,2,1,0:T(2,128)(2,1)S(1)} %get-tuple-element.80), channel_id=1, source_target_pairs={{0,2},{1,3},{2,4},{3,5},{4,6},{5,7},{8,10},{9,11},{10,12},{11,13},... | collective-permute-start | bytes 49160 | tf_op jit(solution)/shard_map/ppermute | solution.py:18
  71.2 5.8 %collective-permute-start.5 = (bf16[2,32,1,128]{3,2,1,0:T(2,128)(2,1)S(1)}, bf16[2,32,1,128]{3,2,1,0:T(2,128)(2,1)S(1)}, u32[]{:S(2)}, u32[]{:S(2)}) collective-permute-start(bf16[2,32,1,128]{3,2,1,0:T(2,128)(2,1)S(1)} %get-tuple-element.81), channel_id=1, source_target_pairs={{2,0},{3,1},{4,2},{5,3},{6,4},{7,5},{10,8},{11,9},{12,10},{13,11},... | collective-permute-start | bytes 49160 | tf_op jit(solution)/shard_map/ppermute | solution.py:18
  77.2 10.8 %copy-start.92 = (f32[256]{0:T(256)S(1)}, f32[256]{0:T(256)}, u32[]{:S(2)}) copy-start(f32[256]{0:T(256)} %param.11) | copy-start | bytes 3076
  77.3 21.0 %copy-start.56 = (bf16[1,1,1,8,32,256]{5,4,3,2,1,0:T(8,128)(2,1)S(1)}, bf16[1,1,1,8,32,256]{5,4,3,2,1,0:T(8,128)(2,1)}, u32[]{:S(2)}) copy-start(bf16[1,1,1,8,32,256]{5,4,3,2,1,0:T(8,128)(2,1)} %param.13) | copy-start | bytes 393220
  77.3 21.0 %copy-start.93 = (bf16[256,256]{1,0:T(8,128)(2,1)S(1)}, bf16[256,256]{1,0:T(8,128)(2,1)}, u32[]{:S(2)}) copy-start(bf16[256,256]{1,0:T(8,128)(2,1)} %param.12) | copy-start | bytes 393220
  78.2 5.4 %collective-permute-start.6 = (f32[128]{0:T(128)S(1)}, f32[128]{0:T(128)S(1)}, u32[]{:S(2)}, u32[]{:S(2)}) collective-permute-start(f32[128]{0:T(128)S(1)} %get-tuple-element.44), channel_id=1, source_target_pairs={{6,0},{7,1},{0,2},{1,3},{2,4},{3,5},{4,6},{5,7},{14,8},{15,9},{8,1... | collective-permute-start | bytes 1544 | tf_op jit(solution)/shard_map/ppermute | solution.py:12
  83.6 4.4 %collective-permute-start.7 = (f32[128]{0:T(128)S(1)}, f32[128]{0:T(128)S(1)}, u32[]{:S(2)}, u32[]{:S(2)}) collective-permute-start(f32[128]{0:T(128)S(1)} %add.365), channel_id=1, source_target_pairs={{4,0},{5,1},{6,2},{7,3},{0,4},{1,5},{2,6},{3,7},{12,8},{13,9},{14,... | collective-permute-start | bytes 1544 | tf_op jit(solution)/shard_map/ppermute | solution.py:12
  108.8 5.4 %collective-permute-start.8 = (f32[128]{0:T(128)S(1)}, f32[128]{0:T(128)S(1)}, u32[]{:S(2)}, u32[]{:S(2)}) collective-permute-start(f32[128]{0:T(128)S(1)} %fusion.67), channel_id=1, source_target_pairs={{6,0},{7,1},{0,2},{1,3},{2,4},{3,5},{4,6},{5,7},{14,8},{15,9},{8,1... | collective-permute-start | bytes 1544 | tf_op jit(solution)/shard_map/ppermute | solution.py:12
  114.3 9.1 %copy-start.90 = (f32[256]{0:T(256)}, f32[256]{0:T(256)S(1)}, u32[]{:S(2)}) copy-start(f32[256]{0:T(256)S(1)} %get-tuple-element.109) | copy-start | bytes 3076
  114.3 4.5 %collective-permute-start.9 = (f32[128]{0:T(128)S(1)}, f32[128]{0:T(128)S(1)}, u32[]{:S(2)}, u32[]{:S(2)}) collective-permute-start(f32[128]{0:T(128)S(1)} %get-tuple-element.110), channel_id=1, source_target_pairs={{4,0},{5,1},{6,2},{7,3},{0,4},{1,5},{2,6},{3,7},{12,8},{13,9},{14,... | collective-permute-start | bytes 1544 | tf_op jit(solution)/shard_map/ppermute | solution.py:12
  118.7 8.7 %copy-start.67 = (f32[128]{0:T(128)S(1)}, f32[128]{0:T(128)}, u32[]{:S(2)}) copy-start(f32[128]{0:T(128)} %copy-done.66) | copy-start | bytes 1540
  120.1 3.3 %collective-permute-start.10 = (bf16[2,32,1,128]{3,2,1,0:T(2,128)(2,1)S(1)}, bf16[2,32,1,128]{3,2,1,0:T(2,128)(2,1)S(1)}, u32[]{:S(2)}, u32[]{:S(2)}) collective-permute-start(bf16[2,32,1,128]{3,2,1,0:T(2,128)(2,1)S(1)} %get-tuple-element.78), channel_id=1, source_target_pairs={{0,2},{1,3},{2,4},{3,5},{4,6},{5,7},{8,10},{9,11},{10,12},{11,13},... | collective-permute-start | bytes 49160 | tf_op jit(solution)/shard_map/ppermute | solution.py:18
  121.4 5.8 %collective-permute-start.11 = (bf16[2,32,1,128]{3,2,1,0:T(2,128)(2,1)S(1)}, bf16[2,32,1,128]{3,2,1,0:T(2,128)(2,1)S(1)}, u32[]{:S(2)}, u32[]{:S(2)}) collective-permute-start(bf16[2,32,1,128]{3,2,1,0:T(2,128)(2,1)S(1)} %get-tuple-element.79), channel_id=1, source_target_pairs={{2,0},{3,1},{4,2},{5,3},{6,4},{7,5},{10,8},{11,9},{12,10},{13,11},... | collective-permute-start | bytes 49160 | tf_op jit(solution)/shard_map/ppermute | solution.py:18
  129.0 11.4 %all-to-all-start.3 = ((bf16[8,1,8,8,128]{4,3,2,1,0:T(8,128)(2,1)}), bf16[8,1,8,8,128]{4,3,2,1,0:T(8,128)(2,1)}, u32[]{:S(2)}, u32[]{:S(2)}) async-start(bf16[8,1,8,8,128]{4,3,2,1,0:T(8,128)(2,1)} %bitcast.533), calls=%async_computation.3 | async-start | bytes 262144 | tf_op jit(solution)/shard_map/all_to_all | solution.py:171
  133.0 159.1 %all-reduce.7.cloned.1.call-start = ((), (), s32[]{:S(2)}) async-start(), calls=%async_computation.4 | async-start | bytes 6160384 | tf_op jit(solution)/shard_map/psum | solution.py:217
  (78 other events, 219.5 us)
Sparse Core Ops, SparseCore 0:
  155.9 136.2 all-reduce.6
where the time goes:
time: 305 us; the launch traced here: 304 us
  waiting for transfers between devices  150 us (49%)
  blocking collectives  59.4 us (19%)
  starting transfers between devices  26.2 us (9%)
  matrix products  22.7 us (7%)
  local copies, waits for them, and re-layouts  20.5 us (7%)
  between operations  15.6 us (5%)
  other arithmetic  9.03 us (3%)
    psum x1, waiting for transfers between devices, local(): lax.psum((grad_fine, grad_down, depth_part, gain_part, grad_point), ('dp'...  94 us
    psum x1, blocking collectives, local(): lax.psum((grad_fine, grad_down, depth_part, gain_part, grad_point), ('dp'...  39.6 us
    ppermute x8, waiting for transfers between devices, shifted_2(): return lax.ppermute(value, axis, pairs)  26.5 us
    ppermute x4, waiting for transfers between devices, shifted(): return lax.ppermute(block, axis, route)  18.4 us
    ppermute x8, starting transfers between devices, shifted_2(): return lax.ppermute(value, axis, pairs)  17.6 us
    all_to_all x1, blocking collectives, to_brick(): lax.all_to_all(parts, 'space', split_axis=0, concat_axis=0, tiled=True)  10 us
    all_to_all x1, blocking collectives, to_local(): lax.all_to_all(parts, 'space', split_axis=0, concat_axis=0, tiled=True)  9.74 us
    unnamed x193, local copies, waits for them, and re-layouts  9.55 us
  transfers between devices with their start and end apart: 15, of which 13 were waited for; matrix products, arithmetic and copies ran while one was open for 2% of the time, Pallas kernels for 0%

commit v1 on v0

v1 whole, which is shorter than its diff:
```python
import functools
import jax
import jax.numpy as jnp
from jax import lax
from jax.experimental import pallas as pl
from jax.experimental.pallas import tpu as pltpu
from jax.sharding import PartitionSpec as P

eps = 1e-05
MESH = pl.DeviceIdType.MESH
OFFSETS = [(dx, dy) for dx in (-1, 0, 1) for dy in (-1, 0, 1) if (dx, dy) != (0, 0)]
VMEM_SPEC = pl.BlockSpec(memory_space=pltpu.VMEM)
VMEM_BYTES = 40 * 1024 * 1024


def tap_offsets(tap_index):
    return (tap_index // 9, tap_index // 3 % 3, tap_index % 3)


def full_conv(padded, w_taps):
    ext_x, ext_y, ext_z = (padded.shape[0] - 2, padded.shape[1] - 2, padded.shape[2] - 2)
    summed = jnp.zeros((ext_x * ext_y * ext_z, w_taps.shape[2]), jnp.float32)
    for tap_index in range(27):
        shift_x, shift_y, shift_z = tap_offsets(tap_index)
        window = padded[
            shift_x : shift_x + ext_x, shift_y : shift_y + ext_y, shift_z : shift_z + ext_z
        ].reshape(-1, padded.shape[3])
        summed = summed + jnp.dot(window, w_taps[tap_index], preferred_element_type=jnp.float32)
    return summed


def tap_grads(padded, grad_rows):
    ext_x, ext_y, ext_z = (padded.shape[0] - 2, padded.shape[1] - 2, padded.shape[2] - 2)
    result = []
    for tap_index in range(27):
        shift_x, shift_y, shift_z = tap_offsets(tap_index)
        window = padded[
            shift_x : shift_x + ext_x, shift_y : shift_y + ext_y, shift_z : shift_z + ext_z
        ].reshape(-1, padded.shape[3])
        result.append(
            lax.dot_general(
                window, grad_rows, (((0,), (0,)), ((), ())), preferred_element_type=jnp.float32
            )
        )
    return jnp.stack(result)


def to_blocks(grid):
    ext_x, ext_y, ext_z, chans = grid.shape
    split = grid.reshape(ext_x // 2, 2, ext_y // 2, 2, ext_z // 2, 2, chans)
    return split.transpose(0, 2, 4, 1, 3, 5, 6).reshape(-1, 8 * chans)


def from_blocks(rows, ext_x, ext_y, ext_z, chans):
    split = rows.reshape(ext_x // 2, ext_y // 2, ext_z // 2, 2, 2, 2, chans)
    return split.transpose(0, 3, 1, 4, 2, 5, 6).reshape(-1, chans)


def silu_slope(value):
    sigma = jax.nn.sigmoid(value)
    return sigma * (1.0 + value * (1.0 - sigma))


def greet_sample(nodes):
    me, dp = lax.axis_index("space"), lax.axis_index("dp")
    barrier = pltpu.get_barrier_semaphore()
    for step in range(1, nodes):
        peer = lax.rem(me + step, nodes)
        pl.semaphore_signal(barrier, inc=1, device_id=(dp, peer), device_id_type=MESH)
    pl.semaphore_wait(barrier, nodes - 1)


def edge_of(delta, ext):
    return {-1: pl.ds(0, 1), 0: pl.ds(0, ext), 1: pl.ds(ext - 1, 1)}[delta]


def rim_of(delta, ext):
    return {-1: pl.ds(0, 1), 0: pl.ds(1, ext), 1: pl.ds(ext + 1, 1)}[delta]


def halo_copies(src, dst, send_sem, recv_sem, nodes):
    me, dp = lax.axis_index("space"), lax.axis_index("dp")
    ext_x, ext_y = src.shape[0], src.shape[1]
    pos_x, pos_y = me // 4, lax.rem(me, 4)
    result = []
    for k, (dx, dy) in enumerate(OFFSETS):
        exists = jnp.logical_and(
            jnp.logical_and(pos_x + dx >= 0, pos_x + dx < nodes // 4),
            jnp.logical_and(pos_y + dy >= 0, pos_y + dy < 4),
        )
        source = src.at[edge_of(dx, ext_x), edge_of(dy, ext_y)]
        peer = (dp, me + 4 * dx + dy)
        send = pltpu.make_async_remote_copy(
            src_ref=source,
            dst_ref=dst.at[rim_of(-dx, ext_x), rim_of(-dy, ext_y)],
            send_sem=send_sem.at[k],
            recv_sem=recv_sem.at[7 - k],
            device_id=peer,
            device_id_type=MESH,
        )
        arrival = pltpu.make_async_remote_copy(
            src_ref=source,
            dst_ref=dst.at[rim_of(dx, ext_x), rim_of(dy, ext_y)],
            send_sem=send_sem.at[k],
            recv_sem=recv_sem.at[k],
            device_id=peer,
            device_id_type=MESH,
        )
        result.append((exists, send, arrival))
    return result


def start_all(copies):
    for exists, send, _ in copies:
        pl.when(exists)(send.start)


def finish_all(copies):
    for exists, _, arrival in copies:
        pl.when(exists)(arrival.wait)


def halo_kernel(nodes, src, out, send_sem, recv_sem):
    ext_x, ext_y = src.shape[0], src.shape[1]
    out[...] = jnp.zeros_like(out)
    greet_sample(nodes)
    copies = halo_copies(src, out, send_sem, recv_sem, nodes)
    start_all(copies)
    out[pl.ds(1, ext_x), pl.ds(1, ext_y)] = src[...]
    finish_all(copies)


def fine_halo(fine, nodes):
    ext_x, ext_y, ext_z, chans = fine.shape
    return pl.pallas_call(
        functools.partial(halo_kernel, nodes),
        out_shape=jax.ShapeDtypeStruct((ext_x + 2, ext_y + 2, ext_z, chans), fine.dtype),
        in_specs=[VMEM_SPEC],
        out_specs=VMEM_SPEC,
        scratch_shapes=[pltpu.SemaphoreType.DMA((8,)), pltpu.SemaphoreType.DMA((8,))],
        compiler_params=pltpu.CompilerParams(
            collective_id=0, has_side_effects=True, vmem_limit_bytes=VMEM_BYTES
        ),
        name="fine_halo",
    )(fine)


def fold8(rows):
    return jnp.sum(rows.reshape(rows.shape[0] // 8, 8, rows.shape[1]), axis=0)


def spread_copies(own, slots, send_sem, recv_sem, nodes):
    me, dp = lax.axis_index("space"), lax.axis_index("dp")
    return [
        pltpu.make_async_remote_copy(
            src_ref=own,
            dst_ref=slots.at[step],
            send_sem=send_sem.at[step],
            recv_sem=recv_sem.at[step],
            device_id=(dp, lax.rem(me + step, nodes)),
            device_id_type=MESH,
        )
        for step in range(1, nodes)
    ]


def fill_grid(grid, padded):
    ext_z = padded.shape[2]
    side = jnp.zeros(grid.shape[:2] + (8, grid.shape[3]), jnp.float32)
    grid[:, :, pl.ds(0, 8)] = side
    grid[:, :, pl.ds(8 + ext_z, 8)] = side
    grid[:, :, pl.ds(8, ext_z)] = padded[...].astype(jnp.float32)


def coarse_kernel(
    nodes, coarse, up, depth_w, gain_ref, point_w,
    out, grad_coarse, grad_point, grad_depth, grad_gain,
    c_pad, g_pad, g_own, c_grid, g_grid, depth_out, g_act,
    own_1, own_2, slots_1, slots_2,
    sem_a, sem_b, sem_c, sem_d, sem_e, sem_f, sem_g, sem_h,
):
    ext_x, ext_y, ext_z, chans = coarse.shape
    cells = ext_x * ext_y * ext_z
    count = nodes * cells
    c_pad[...] = jnp.zeros_like(c_pad)
    g_pad[...] = jnp.zeros_like(g_pad)
    greet_sample(nodes)
    first = halo_copies(coarse, c_pad, sem_a, sem_b, nodes)
    start_all(first)
    c_pad[pl.ds(1, ext_x), pl.ds(1, ext_y)] = coarse[...]
    up_rows = up[...].reshape(cells, chans)
    g_act[...] = lax.dot_general(
        up_rows, point_w[...], (((1,), (1,)), ((), ())), preferred_element_type=jnp.float32
    )
    finish_all(first)
    fill_grid(c_grid, c_pad)

    def conv_row(grid, x, y, flip):
        total = None
        for t in range(27):
            a, b, c = tap_offsets(t)
            w_at = 26 - t if flip else t
            term = grid[x + a, y + b, pl.ds(7 + c, ext_z), :] * depth_w[pl.ds(w_at, 1), :]
            total = term if total is None else total + term
        return total

    squares = jnp.zeros((8, chans), jnp.float32)
    for x in range(ext_x):
        def forward(y, acc):
            row = conv_row(c_grid, x, y, False)
            depth_out[pl.ds(pl.multiple_of((x * ext_y + y) * ext_z, ext_z), ext_z), :] = row
            return acc + fold8(row * row)
        squares = lax.fori_loop(0, ext_y, forward, squares)
    own_1[...] = squares
    spread_1 = spread_copies(own_1, slots_1, sem_c, sem_d, nodes)
    for copy in spread_1:
        copy.start()
    for copy in spread_1:
        copy.wait()
    total = own_1[...]
    for step in range(1, nodes):
        total = total + slots_1[step]
    square_sum = jnp.sum(total, axis=0, keepdims=True)
    gain = gain_ref[...]
    scale = lax.rsqrt(square_sum / count + eps)
    depth_all = depth_out[...]
    normed = (depth_all * (gain * scale)).astype(jnp.bfloat16).astype(jnp.float32)
    sigma = jax.nn.sigmoid(normed)
    activated = (normed * sigma).astype(jnp.bfloat16)
    slope = sigma * (1.0 + normed * (1.0 - sigma))
    g_normed = (g_act[...] * slope).astype(jnp.bfloat16).astype(jnp.float32)
    g_act[...] = g_normed
    own_2[...] = fold8(g_normed * depth_all)
    spread_2 = spread_copies(own_2, slots_2, sem_e, sem_f, nodes)
    for copy in spread_2:
        copy.start()
    mixed = coarse[...].reshape(cells, chans).astype(jnp.float32) + jnp.dot(
        activated, point_w[...], preferred_element_type=jnp.float32
    )
    out[...] = mixed.astype(jnp.bfloat16).reshape(coarse.shape)
    grad_point[...] = lax.dot_general(
        activated, up_rows, (((0,), (0,)), ((), ())), preferred_element_type=jnp.float32
    )
    grad_gain[...] = scale * jnp.sum(own_2[...], axis=0, keepdims=True)
    for copy in spread_2:
        copy.wait()
    total = own_2[...]
    for step in range(1, nodes):
        total = total + slots_2[step]
    cross = jnp.sum(total, axis=0, keepdims=True)
    g_in = gain * scale * g_act[...] - depth_out[...] * (
        gain * scale * scale * scale / count
    ) * cross
    g_own[...] = g_in.astype(jnp.bfloat16).reshape(coarse.shape)
    second = halo_copies(g_own, g_pad, sem_g, sem_h, nodes)
    start_all(second)
    g_pad[pl.ds(1, ext_x), pl.ds(1, ext_y)] = g_own[...]
    for a in range(3):
        sums = tuple(jnp.zeros((8, chans), jnp.float32) for _ in range(9))
        for x in range(ext_x):
            def taps(y, acc):
                g_row = g_own[x, y].astype(jnp.float32)
                return tuple(
                    acc[3 * b + c] + fold8(c_grid[x + a, y + b, pl.ds(7 + c, ext_z), :] * g_row)
                    for b in range(3)
                    for c in range(3)
                )
            sums = lax.fori_loop(0, ext_y, taps, sums)
        for k in range(9):
            grad_depth[pl.ds(9 * a + k, 1), :] = jnp.sum(sums[k], axis=0, keepdims=True)
    finish_all(second)
    fill_grid(g_grid, g_pad)
    for x in range(ext_x):
        def backward(y, carry):
            row = conv_row(g_grid, x, y, True).astype(jnp.bfloat16).astype(jnp.float32)
            grad_coarse[x, y] = (up[x, y].astype(jnp.float32) + row).astype(jnp.bfloat16)
            return carry
        lax.fori_loop(0, ext_y, backward, 0)


def coarse_level(coarse, up, depth_w, gain, point_w, nodes):
    ext_x, ext_y, ext_z, chans = coarse.shape
    cells = ext_x * ext_y * ext_z
    f32, bf16 = jnp.float32, jnp.bfloat16
    padded = (ext_x + 2, ext_y + 2, ext_z, chans)
    grid = (ext_x + 2, ext_y + 2, ext_z + 16, chans)
    dma = pltpu.SemaphoreType.DMA
    return pl.pallas_call(
        functools.partial(coarse_kernel, nodes),
        out_shape=(
            jax.ShapeDtypeStruct(coarse.shape, bf16),
            jax.ShapeDtypeStruct(coarse.shape, bf16),
            jax.ShapeDtypeStruct((chans, chans), f32),
            jax.ShapeDtypeStruct((27, chans), f32),
            jax.ShapeDtypeStruct((1, chans), f32),
        ),
        in_specs=[VMEM_SPEC] * 5,
        out_specs=(VMEM_SPEC,) * 5,
        scratch_shapes=[
            pltpu.VMEM(padded, bf16),
            pltpu.VMEM(padded, bf16),
            pltpu.VMEM(coarse.shape, bf16),
            pltpu.VMEM(grid, f32),
            pltpu.VMEM(grid, f32),
            pltpu.VMEM((cells, chans), f32),
            pltpu.VMEM((cells, chans), f32),
            pltpu.VMEM((8, chans), f32),
            pltpu.VMEM((8, chans), f32),
            pltpu.VMEM((nodes, 8, chans), f32),
            pltpu.VMEM((nodes, 8, chans), f32),
            dma((8,)), dma((8,)), dma((nodes,)), dma((nodes,)),
            dma((nodes,)), dma((nodes,)), dma((8,)), dma((8,)),
        ],
        compiler_params=pltpu.CompilerParams(
            collective_id=1, has_side_effects=True, vmem_limit_bytes=VMEM_BYTES
        ),
        name="coarse_level",
    )(coarse, up, depth_w, gain.reshape(1, chans), point_w)


def sum_kernel(nodes, src, out, got_1, got_2, got_3, part_1, part_2,
               core_send, core_recv, plane_send, plane_recv, line_send, line_recv):
    chunks, _, plane = src.shape[:3]
    width = nodes // 4
    me, dp = lax.axis_index("space"), lax.axis_index("dp")
    core = lax.rem(dp, 2)
    line, q = me // width, (dp // 2) * width + lax.rem(me, width)
    mate = (dp + 1 - 2 * core, me)

    def in_plane(step):
        at = lax.rem(q + step, plane)
        return at, ((at // width) * 2 + core, line * width + lax.rem(at, width))

    def in_line(step):
        at = lax.rem(line + step, 4)
        return at, (dp, at * width + lax.rem(me, width))

    barrier = pltpu.get_barrier_semaphore()
    peers = [mate] + [in_plane(s)[1] for s in range(1, plane)] + [in_line(s)[1] for s in range(1, 4)]
    for peer in peers:
        pl.semaphore_signal(barrier, inc=1, device_id=peer, device_id_type=MESH)
    pl.semaphore_wait(barrier, len(peers))

    def copy(source, dest, send_sem, recv_sem, peer):
        made = pltpu.make_async_remote_copy(
            src_ref=source, dst_ref=dest, send_sem=send_sem, recv_sem=recv_sem,
            device_id=peer, device_id_type=MESH,
        )
        made.start()
        return made

    f32, bf16 = jnp.float32, jnp.bfloat16
    sent = []

    def arrived(source, dest, send_sem, recv_sem, peer):
        pltpu.make_async_remote_copy(
            src_ref=source, dst_ref=dest, send_sem=send_sem, recv_sem=recv_sem,
            device_id=peer, device_id_type=MESH,
        ).wait_recv()

    step_1 = []
    for c in range(chunks):
        step_1.append(copy(src.at[c, 1 - core], got_1.at[c], core_send.at[0, c],
                           core_recv.at[0, c], mate))
    step_2 = []
    for c in range(chunks):
        step_1[c].wait()
        part_1[c] = (src[c, core].astype(f32) + got_1[c].astype(f32)).astype(bf16)
        row = []
        for s in range(1, plane):
            at, peer = in_plane(s)
            row.append(copy(part_1.at[c, at], got_2.at[c, s], plane_send.at[0, c, s],
                            plane_recv.at[0, c, s], peer))
        step_2.append(row)
    step_3 = []
    for c in range(chunks):
        for made in step_2[c]:
            made.wait()
        total = part_1[c, q].astype(f32)
        for s in range(1, plane):
            total = total + got_2[c, s].astype(f32)
        part_2[c] = total.astype(bf16)
        row = []
        for s in range(1, 4):
            at, peer = in_line(s)
            row.append(copy(part_2.at[c, at], got_3.at[c, s], line_send.at[0, c, s],
                            line_recv.at[0, c, s], peer))
        step_3.append(row)
    for c in range(chunks):
        for made in step_3[c]:
            made.wait()
        total = part_2[c, line].astype(f32)
        for s in range(1, 4):
            total = total + got_3[c, s].astype(f32)
        out[c, core, q, line] = total.astype(bf16)
        for s in range(1, 4):
            peer = in_line(s)[1]
            mine = out.at[c, core, q, line]
            sent.append(copy(mine, mine, line_send.at[1, c, s], line_recv.at[1, c, s], peer))
    for c in range(chunks):
        for s in range(1, 4):
            at, peer = in_line(4 - s)
            there = out.at[c, core, q, at]
            arrived(there, there, line_send.at[1, c, s], line_recv.at[1, c, s], peer)
        for s in range(1, plane):
            peer = in_plane(s)[1]
            mine = out.at[c, core, q]
            sent.append(copy(mine, mine, plane_send.at[1, c, s], plane_recv.at[1, c, s], peer))
    for c in range(chunks):
        for s in range(1, plane):
            at, peer = in_plane(plane - s)
            there = out.at[c, core, at]
            arrived(there, there, plane_send.at[1, c, s], plane_recv.at[1, c, s], peer)
        mine = out.at[c, core]
        sent.append(copy(mine, mine, core_send.at[1, c], core_recv.at[1, c], mate))
    for c in range(chunks):
        there = out.at[c, 1 - core]
        arrived(there, there, core_send.at[1, c], core_recv.at[1, c], mate)
    for made in sent:
        made.wait_send()


CHUNKS = 3


def sum_everywhere(grads, nodes, groups):
    plane = groups // 2 * (nodes // 4)
    lane = 128
    unit = CHUNKS * 2 * plane * 4 * 16
    flat = []
    for grad in grads:
        flat.append(grad.astype(jnp.bfloat16).reshape(-1, lane))
    rows = sum(part.shape[0] for part in flat)
    padded = -(-rows // unit) * unit
    if padded > rows:
        flat.append(jnp.zeros((padded - rows, lane), jnp.bfloat16))
    piece = padded // (CHUNKS * 2 * plane * 4)
    whole = jnp.concatenate(flat, axis=0).reshape(CHUNKS, 2, plane, 4, piece, lane)
    bf16, dma = jnp.bfloat16, pltpu.SemaphoreType.DMA
    summed = pl.pallas_call(
        functools.partial(sum_kernel, nodes),
        out_shape=jax.ShapeDtypeStruct(whole.shape, bf16),
        in_specs=[VMEM_SPEC],
        out_specs=VMEM_SPEC,
        scratch_shapes=[
            pltpu.VMEM((CHUNKS, plane, 4, piece, lane), bf16),
            pltpu.VMEM((CHUNKS, plane, 4, piece, lane), bf16),
            pltpu.VMEM((CHUNKS, 4, piece, lane), bf16),
            pltpu.VMEM((CHUNKS, plane, 4, piece, lane), bf16),
            pltpu.VMEM((CHUNKS, 4, piece, lane), bf16),
            dma((2, CHUNKS)), dma((2, CHUNKS)),
            dma((2, CHUNKS, plane)), dma((2, CHUNKS, plane)),
            dma((2, CHUNKS, 4)), dma((2, CHUNKS, 4)),
        ],
        compiler_params=pltpu.CompilerParams(
            collective_id=2, has_side_effects=True, vmem_limit_bytes=VMEM_BYTES
        ),
        name="sum_everywhere",
    )(whole).reshape(padded, lane)
    result, at = [], 0
    for grad in grads:
        count = grad.size // lane
        result.append(summed[at : at + count].astype(jnp.float32).reshape(grad.shape))
        at += count
    return result


def local(fields, conv_fine, conv_down, conv_depth, norm_gain, conv_point, upstream):
    nodes, groups = lax.axis_size("space"), lax.axis_size("dp")
    fine = fields[0, 0]
    brick_x, brick_y, brick_z, chan_fine = fine.shape
    fine_pad = jnp.pad(fine_halo(fine, nodes), ((0, 0), (0, 0), (1, 1), (0, 0)))
    pre_act = full_conv(fine_pad, conv_fine)
    act = jax.nn.silu(pre_act).astype(jnp.bfloat16)
    blocks = to_blocks(act.reshape(brick_x, brick_y, brick_z, chan_fine))
    coarse = jnp.dot(blocks, conv_down, preferred_element_type=jnp.float32).astype(jnp.bfloat16)
    up = upstream[0, 0]
    coarse_out, grad_coarse, grad_point, grad_depth, grad_gain = coarse_level(
        coarse.reshape(up.shape), up, conv_depth, norm_gain, conv_point, nodes
    )
    grad_coarse = grad_coarse.reshape(-1, up.shape[3])
    grad_down = lax.dot_general(
        blocks, grad_coarse, (((0,), (0,)), ((), ())), preferred_element_type=jnp.float32
    )
    grad_blocks = lax.dot_general(
        grad_coarse, conv_down, (((1,), (1,)), ((), ())), preferred_element_type=jnp.float32
    )
    grad_act_fine = from_blocks(grad_blocks, brick_x, brick_y, brick_z, chan_fine)
    grad_pre = (grad_act_fine * silu_slope(pre_act)).astype(jnp.bfloat16)
    grad_fine = tap_grads(fine_pad, grad_pre)
    totals = sum_everywhere(
        (grad_fine, grad_down, grad_depth, grad_gain.reshape(-1), grad_point), nodes, groups
    )
    return (coarse_out[None, None], *totals)


def solution(mesh):
    placed = (
        P("dp", "space", None, None, None, None),
        P(),
        P(),
        P(),
        P(),
        P(),
        P("dp", "space", None, None, None, None),
    )
    return jax.shard_map(
        local,
        mesh=mesh,
        in_specs=placed,
        out_specs=(P("dp", "space", None, None, None, None), P(), P(), P(), P(), P()),
        check_vma=False,
    )
```

time: 305 us -> 136 us (0.45)
  waiting for transfers between devices: 150 us -> 0 us
  Pallas kernels: 0 us -> 79.3 us
  blocking collectives: 59.4 us -> 0 us
  starting transfers between devices: 26.2 us -> 0 us
  between operations: 15.6 us -> 1.48 us
  local copies, waits for them, and re-layouts: 20.5 us -> 28.7 us
  other arithmetic: 9.03 us -> 4.49 us
    psum x1 -> x0, waiting for transfers between devices: 94 us -> none  [local(): lax.psum((grad_fine, grad_down, depth_part, gain_part, grad_point), ('dp'...]
    pallas_call x0 -> x3, Pallas kernels: none -> 79.3 us  [the longest x1 30.7 us: sum_everywhere(): pl.pallas_call(functools.partial(sum_kernel, nodes), out_shape=jax.ShapeD...]
    ppermute x12 -> x0, waiting for transfers between devices: 44.9 us -> none  [the longest x8 26.5 us: shifted_2(): return lax.ppermute(value, axis, pairs)]
    psum x1 -> x0, blocking collectives: 39.6 us -> none  [local(): lax.psum((grad_fine, grad_down, depth_part, gain_part, grad_point), ('dp'...]
    all_to_all x2 -> x0, blocking collectives: 19.8 us -> none  [the longest x1 10 us: to_brick(): lax.all_to_all(parts, 'space', split_axis=0, concat_axis=0, tiled=True)]
    ppermute x12 -> x0, starting transfers between devices: 18.8 us -> none  [the longest x8 17.6 us: shifted_2(): return lax.ppermute(value, axis, pairs)]
    all_to_all x2 -> x0, waiting for transfers between devices: 11.5 us -> none  [the longest x1 6.05 us: to_local(): lax.all_to_all(parts, 'space', split_axis=0, concat_axis=0, tiled=True)]
    all_to_all x2 -> x0, starting transfers between devices: 7.37 us -> none  [the longest x1 4 us: to_brick(): lax.all_to_all(parts, 'space', split_axis=0, concat_axis=0, tiled=True)]
  transfers between devices with their start and end apart: 15 -> 0, of which waited for: 13 -> 0; matrix products, arithmetic and copies ran while one was open for 2% -> 0% of each run, Pallas kernels for 0% -> 0%
where the time goes in v1:
time: 136 us; the launch traced here: 135 us
  Pallas kernels  79.3 us (58%)
  local copies, waits for them, and re-layouts  28.7 us (21%)
  matrix products  21.1 us (16%)
  other arithmetic  4.49 us (3%)
  between operations  1.48 us (1%)
    pallas_call x1, Pallas kernels, sum_everywhere(): pl.pallas_call(functools.partial(sum_kernel, nodes), out_shape=jax.ShapeD...  30.7 us
    pallas_call x1, Pallas kernels, coarse_level(): pl.pallas_call(functools.partial(coarse_kernel, nodes), out_shape=(jax.Sh...  29.3 us
    pallas_call x1, Pallas kernels, fine_halo(): pl.pallas_call(functools.partial(halo_kernel, nodes), out_shape=jax.Shape...  19.3 us
    unnamed x121, local copies, waits for them, and re-layouts  10.3 us
    dot_general x27, matrix products, tap_grads(): lax.dot_general(window, grad_rows, (((0,), (0,)), ((), ())), preferred_el...  9.68 us
    dot_general x27, matrix products, full_conv(): jnp.dot(window, w_taps[tap_index], preferred_element_type=jnp.float32)  8.57 us
    slice x3, local copies, waits for them, and re-layouts, full_conv(): padded[shift_x:shift_x + ext_x, shift_y:shift_y + ext_y, shift_z:shift_z...  4.13 us
    reshape x5, other arithmetic, sum_everywhere(): result.append(summed[at:at + count].astype(jnp.float32).reshape(grad.shape))  4.06 us

profile of v1, /device:TPU:0, one launch (start us, length us, event | category | flops | bytes accessed | tf_op | source)
XLA Modules:
  0.0 135.2 jit_solution(12361484547835428315)
XLA Ops:
  0.6 1.0 copy-done
  1.7 1.0 copy-done.2
  2.7 19.3 %fine_halo.1 = bf16[4,18,64,128]{3,2,1,0:T(8,128)(2,1)S(1)} custom-call(bf16[2,16,64,128]{3,2,1,0:T(8,128)(2,1)S(1)} %bitcast.366), custom_call_target="tpu_custom_call" | custom-call | tf_op jit(solution)/shard_map/fine_halo/pallas_call | solution.py:135
  22.1 0.8 fusion.111
  22.9 0.7 copy-done.24
  24.2 1.4 %pad_slice_fusion = (bf16[2,16,64,128]{3,2,1,0:T(8,128)(2,1)S(1)}, bf16[2,16,64,128]{3,2,1,0:T(8,128)(2,1)S(1)}, bf16[2,16,64,128]{3,2,1,0:T(8,128)(2,1)S(1)}, b...) fusion(bf16[4,18,64,128]{3,2,1,0:T(8,128)(2,1)S(1)} %fine_halo.1), kind=kLoop, calls=%fused_computation.176 | loop fusion | bytes 6946816 | tf_op jit(solution)/shard_map/slice | solution.py:25
  29.4 2.0 %pad_slice_fusion.1 = (bf16[2,16,64,128]{3,2,1,0:T(8,128)(2,1)S(1)}, bf16[2,16,64,128]{3,2,1,0:T(8,128)(2,1)S(1)}, bf16[2,16,64,128]{3,2,1,0:T(8,128)(2,1)S(1)},...) fusion(bf16[4,18,64,128]{3,2,1,0:T(8,128)(2,1)S(1)} %fine_halo.1), kind=kLoop, calls=%fused_computation.177 | loop fusion | bytes 8519680 | tf_op jit(solution)/shard_map/slice | solution.py:25
  35.4 1.3 multiply_convert_fusion.1
  36.8 1.2 copy.18
  38.0 2.3 %reshape.222 = bf16[256,1024]{1,0:T(8,128)(2,1)} reshape(bf16[1,8,32,2,2,2,128]{6,5,4,3,2,1,0:T(2,128)(2,1)} %bitcast.425) | data formatting | bytes 1048576 | tf_op jit(solution)/shard_map/reshape | solution.py:51
  40.3 1.4 %convolution_convert_fusion.1 = bf16[256,256]{1,0:T(8,128)(2,1)S(1)} fusion(bf16[256,1024]{1,0:T(8,128)(2,1)} %reshape.222, bf16[1024,256]{1,0:T(8,128)(2,1)S(1)} %copy-done), kind=kOutput, calls=%fused_computation.28 | convolution fusion | flops 134283264 | bytes 1179648 | tf_op jit(solution)/shard_map/dot_general | solution.py:476
  41.7 29.3 %coarse_level.1 = (bf16[1,8,32,256]{3,2,1,0:T(8,128)(2,1)S(1)}, bf16[1,8,32,256]{3,2,1,0:T(8,128)(2,1)S(1)}, f32[256,256]{1,0:T(8,128)S(1)}, f32[27,256]{1,0:T(8,128)S(1)}, f32[1,256]{1,0:T(1,128)S(1)}) custom-call(bf16[1,8,32,256]{3,2,1,0:T(8,128)(2,1)S(1)} %bitcast.365, bf16[1,8,32,256]{3,2,1,0:T(8,128)(2,1)S(1)} %bitcast.368, f32[27,256]{1,0:T(8,128)S(1)} %copy-done.5, ...), custom_call_target="tpu_custom_call" | custom-call | tf_op jit(solution)/shard_map/coarse_level/pallas_call | solution.py:288
  71.1 1.1 convolution_convert_fusion
  72.2 2.0 %reshape.228 = bf16[2048,128]{1,0:T(8,128)(2,1)} reshape(bf16[1024,256]{1,0:T(8,128)(2,1)} %convolution_convert_fusion) | data formatting | bytes 1048576 | tf_op jit(solution)/shard_map/reshape | solution.py:432
  74.7 0.8 copy.15
  75.9 0.4 multiply_convert_fusion
  78.8 0.4 fusion.9
  80.3 0.4 fusion.15
  88.2 0.4 fusion.45
  90.4 0.9 copy-done.58
  91.3 4.0 %concatenate.3 = bf16[6144,128]{1,0:T(8,128)(2,1)S(1)} concatenate(bf16[3456,128]{1,0:T(8,128)(2,1)} %bitcast.428, bf16[2048,128]{1,0:T(8,128)(2,1)S(1)} %copy-done.54, bf16[54,128]{1,0:T(8,128)(2,1)S(1)} %reshape.229, bf16[2,128]{1,0:T(2,128)(2,1)S(1)} %bitcast.430, bf16[512,128]{1,0:T(8,128)(2,1)S(1)} %reshape.230, bf16[72,128]{1,0:T(8,128)(2,1)S(1)} %broadcast_in_dim.7), dimensions={0} | concatenate | bytes 3145728 | tf_op jit(solution)/shard_map/concatenate | solution.py:438
  95.4 30.7 %sum_everywhere.1 = bf16[3,2,4,4,64,128]{5,4,3,2,1,0:T(8,128)(2,1)S(1)} custom-call(bf16[3,2,4,4,64,128]{5,4,3,2,1,0:T(8,128)(2,1)S(1)} %bitcast.359), custom_call_target="tpu_custom_call" | custom-call | tf_op jit(solution)/shard_map/sum_everywhere/pallas_call | solution.py:440
  126.0 0.6 fusion.110
  126.6 0.5 copy-done.1
  127.2 0.6 reshape.248
  127.8 0.9 slice_convert_fusion.1
  128.7 0.8 reshape.252
  129.5 1.2 slice.272
  130.7 1.1 slice_convert_fusion
  131.8 1.3 reshape.246
  133.1 1.4 %convert.149 = f32[27,128,128]{2,1,0:T(8,128)} convert(bf16[27,128,128]{2,1,0:T(8,128)(2,1)S(1)} %bitcast.424) | non-fusion elementwise | flops 442368 | bytes 2654208 | tf_op jit(solution)/shard_map/reshape | solution.py:463
  134.5 0.7 copy.46
  (173 shorter events, 21.6 us)
Async XLA Ops:
  22.1 1.6 %copy-start.59 = (bf16[27,128,128]{2,1,0:T(8,128)(2,1)S(1)}, bf16[27,128,128]{2,1,0:T(8,128)(2,1)}, u32[]{:S(2)}) copy-start(bf16[27,128,128]{2,1,0:T(8,128)(2,1)} %param.8) | copy-start | bytes 2654212
  22.9 3.4 %copy-start.40 = (bf16[2,16,64,128]{3,2,1,0:T(8,128)(2,1)}, bf16[2,16,64,128]{3,2,1,0:T(8,128)(2,1)S(1)}, u32[]{:S(2)}) copy-start(bf16[2,16,64,128]{3,2,1,0:T(8,128)(2,1)S(1)} %get-tuple-element.40) | copy-start | bytes 1572868
  22.9 4.5 %copy-start.32 = (bf16[2,16,64,128]{3,2,1,0:T(8,128)(2,1)}, bf16[2,16,64,128]{3,2,1,0:T(8,128)(2,1)S(1)}, u32[]{:S(2)}) copy-start(bf16[2,16,64,128]{3,2,1,0:T(8,128)(2,1)S(1)} %get-tuple-element.39) | copy-start | bytes 1572868
  22.9 5.4 %copy-start.30 = (bf16[2,16,64,128]{3,2,1,0:T(8,128)(2,1)}, bf16[2,16,64,128]{3,2,1,0:T(8,128)(2,1)S(1)}, u32[]{:S(2)}) copy-start(bf16[2,16,64,128]{3,2,1,0:T(8,128)(2,1)S(1)} %get-tuple-element.38) | copy-start | bytes 1572868
  22.9 6.2 %copy-start.28 = (bf16[2,16,64,128]{3,2,1,0:T(8,128)(2,1)}, bf16[2,16,64,128]{3,2,1,0:T(8,128)(2,1)S(1)}, u32[]{:S(2)}) copy-start(bf16[2,16,64,128]{3,2,1,0:T(8,128)(2,1)S(1)} %get-tuple-element.37) | copy-start | bytes 1572868
  25.6 1.2 copy-start.52
  25.6 1.4 %copy-start.44 = (bf16[2,16,64,128]{3,2,1,0:T(8,128)(2,1)}, bf16[2,16,64,128]{3,2,1,0:T(8,128)(2,1)S(1)}, u32[]{:S(2)}) copy-start(bf16[2,16,64,128]{3,2,1,0:T(8,128)(2,1)S(1)} %get-tuple-element.20) | copy-start | bytes 1572868
  25.6 2.0 %copy-start.42 = (bf16[2,16,64,128]{3,2,1,0:T(8,128)(2,1)}, bf16[2,16,64,128]{3,2,1,0:T(8,128)(2,1)S(1)}, u32[]{:S(2)}) copy-start(bf16[2,16,64,128]{3,2,1,0:T(8,128)(2,1)S(1)} %get-tuple-element.21) | copy-start | bytes 1572868
  25.6 2.3 %copy-start.38 = (bf16[2,16,64,128]{3,2,1,0:T(8,128)(2,1)}, bf16[2,16,64,128]{3,2,1,0:T(8,128)(2,1)S(1)}, u32[]{:S(2)}) copy-start(bf16[2,16,64,128]{3,2,1,0:T(8,128)(2,1)S(1)} %get-tuple-element.22) | copy-start | bytes 1572868
  25.7 2.9 %copy-start.36 = (bf16[2,16,64,128]{3,2,1,0:T(8,128)(2,1)}, bf16[2,16,64,128]{3,2,1,0:T(8,128)(2,1)S(1)}, u32[]{:S(2)}) copy-start(bf16[2,16,64,128]{3,2,1,0:T(8,128)(2,1)S(1)} %get-tuple-element.23) | copy-start | bytes 1572868
  25.7 3.2 %copy-start.34 = (bf16[2,16,64,128]{3,2,1,0:T(8,128)(2,1)}, bf16[2,16,64,128]{3,2,1,0:T(8,128)(2,1)S(1)}, u32[]{:S(2)}) copy-start(bf16[2,16,64,128]{3,2,1,0:T(8,128)(2,1)S(1)} %get-tuple-element.24) | copy-start | bytes 1572868
  25.7 9.4 %copy-start.26 = (bf16[2,16,64,128]{3,2,1,0:T(8,128)(2,1)}, bf16[2,16,64,128]{3,2,1,0:T(8,128)(2,1)S(1)}, u32[]{:S(2)}) copy-start(bf16[2,16,64,128]{3,2,1,0:T(8,128)(2,1)S(1)} %get-tuple-element.25) | copy-start | bytes 1572868
  25.7 9.7 %copy-start.55 = (bf16[2,16,64,128]{3,2,1,0:T(8,128)(2,1)}, bf16[2,16,64,128]{3,2,1,0:T(8,128)(2,1)S(1)}, u32[]{:S(2)}) copy-start(bf16[2,16,64,128]{3,2,1,0:T(8,128)(2,1)S(1)} %get-tuple-element.16) | copy-start | bytes 1572868
  31.4 1.1 copy-start.15
  31.4 1.2 copy-start.19
  31.5 1.4 %copy-start.21 = (bf16[2,16,64,128]{3,2,1,0:T(8,128)(2,1)}, bf16[2,16,64,128]{3,2,1,0:T(8,128)(2,1)S(1)}, u32[]{:S(2)}) copy-start(bf16[2,16,64,128]{3,2,1,0:T(8,128)(2,1)S(1)} %get-tuple-element.27) | copy-start | bytes 1572868
  31.5 1.6 %copy-start.13 = (bf16[2,16,64,128]{3,2,1,0:T(8,128)(2,1)}, bf16[2,16,64,128]{3,2,1,0:T(8,128)(2,1)S(1)}, u32[]{:S(2)}) copy-start(bf16[2,16,64,128]{3,2,1,0:T(8,128)(2,1)S(1)} %get-tuple-element.30) | copy-start | bytes 1572868
  31.5 1.9 %copy-start.11 = (bf16[2,16,64,128]{3,2,1,0:T(8,128)(2,1)}, bf16[2,16,64,128]{3,2,1,0:T(8,128)(2,1)S(1)}, u32[]{:S(2)}) copy-start(bf16[2,16,64,128]{3,2,1,0:T(8,128)(2,1)S(1)} %get-tuple-element.35) | copy-start | bytes 1572868
  31.5 2.2 %copy-start.9 = (bf16[2,16,64,128]{3,2,1,0:T(8,128)(2,1)}, bf16[2,16,64,128]{3,2,1,0:T(8,128)(2,1)S(1)}, u32[]{:S(2)}) copy-start(bf16[2,16,64,128]{3,2,1,0:T(8,128)(2,1)S(1)} %get-tuple-element.31) | copy-start | bytes 1572868
  31.5 2.5 %copy-start.7 = (bf16[2,16,64,128]{3,2,1,0:T(8,128)(2,1)}, bf16[2,16,64,128]{3,2,1,0:T(8,128)(2,1)S(1)}, u32[]{:S(2)}) copy-start(bf16[2,16,64,128]{3,2,1,0:T(8,128)(2,1)S(1)} %get-tuple-element.32) | copy-start | bytes 1572868
  38.0 3.7 %copy-start.3 = (bf16[1,1,1,8,32,256]{5,4,3,2,1,0:T(8,128)(2,1)S(1)}, bf16[1,1,1,8,32,256]{5,4,3,2,1,0:T(8,128)(2,1)}, u32[]{:S(2)}) copy-start(bf16[1,1,1,8,32,256]{5,4,3,2,1,0:T(8,128)(2,1)} %param.13) | copy-start | bytes 393220
  38.0 3.7 %copy-start.4 = (bf16[256,256]{1,0:T(8,128)(2,1)S(1)}, bf16[256,256]{1,0:T(8,128)(2,1)}, u32[]{:S(2)}) copy-start(bf16[256,256]{1,0:T(8,128)(2,1)} %point_w.1) | copy-start | bytes 393220
  38.0 3.7 %copy-start.5 = (f32[27,256]{1,0:T(8,128)S(1)}, f32[27,256]{1,0:T(8,128)}, u32[]{:S(2)}) copy-start(f32[27,256]{1,0:T(8,128)} %depth_w.1) | copy-start | bytes 82948
  38.0 3.7 %copy-start.6 = (f32[256]{0:T(256)S(1)}, f32[256]{0:T(256)}, u32[]{:S(2)}) copy-start(f32[256]{0:T(256)} %param.11) | copy-start | bytes 3076
  40.2 30.8 %copy-start.23 = (bf16[256,1024]{1,0:T(8,128)(2,1)S(1)}, bf16[256,1024]{1,0:T(8,128)(2,1)}, u32[]{:S(2)}) copy-start(bf16[256,1024]{1,0:T(8,128)(2,1)} %reshape.222) | copy-start | bytes 1572868
  74.7 1.2 copy-start.57
  75.6 1.1 copy-start.25
  75.9 1.1 copy-start.47
  77.0 1.1 copy-start.51
  89.0 1.1 copy-start.56
  89.6 1.7 %copy-start.54 = (bf16[2048,128]{1,0:T(8,128)(2,1)S(1)}, bf16[2048,128]{1,0:T(8,128)(2,1)}, u32[]{:S(2)}) copy-start(bf16[2048,128]{1,0:T(8,128)(2,1)} %reshape.228) | copy-start | bytes 1572868
  126.0 1.1 copy-start.1
  (28 other events, 29.2 us)

commit v2 on v1

v2 whole, which is shorter than its diff:
```python
import functools
import jax
import jax.numpy as jnp
from jax import lax
from jax.experimental import pallas as pl
from jax.experimental.pallas import tpu as pltpu
from jax.sharding import PartitionSpec as P

eps = 1e-05
MESH = pl.DeviceIdType.MESH
OFFSETS = [(dx, dy) for dx in (-1, 0, 1) for dy in (-1, 0, 1) if (dx, dy) != (0, 0)]
VMEM_SPEC = pl.BlockSpec(memory_space=pltpu.VMEM)
VMEM_BYTES = 48 * 1024 * 1024


def tap_offsets(tap_index):
    return (tap_index // 9, tap_index // 3 % 3, tap_index % 3)


def edge_of(delta, ext):
    return {-1: pl.ds(0, 1), 0: pl.ds(0, ext), 1: pl.ds(ext - 1, 1)}[delta]


def rim_of(delta, ext):
    return {-1: pl.ds(0, 1), 0: pl.ds(1, ext), 1: pl.ds(ext + 1, 1)}[delta]


def halo_copies(src, dst, send_sem, recv_sem, nodes):
    me, dp = lax.axis_index("space"), lax.axis_index("dp")
    ext_x, ext_y = src.shape[0], src.shape[1]
    pos_x, pos_y = me // 4, lax.rem(me, 4)
    result = []
    for k, (dx, dy) in enumerate(OFFSETS):
        exists = jnp.logical_and(
            jnp.logical_and(pos_x + dx >= 0, pos_x + dx < nodes // 4),
            jnp.logical_and(pos_y + dy >= 0, pos_y + dy < 4),
        )
        source = src.at[edge_of(dx, ext_x), edge_of(dy, ext_y)]
        peer = (dp, me + 4 * dx + dy)
        send = pltpu.make_async_remote_copy(
            src_ref=source,
            dst_ref=dst.at[rim_of(-dx, ext_x), rim_of(-dy, ext_y)],
            send_sem=send_sem.at[k],
            recv_sem=recv_sem.at[7 - k],
            device_id=peer,
            device_id_type=MESH,
        )
        arrival = pltpu.make_async_remote_copy(
            src_ref=source,
            dst_ref=dst.at[rim_of(dx, ext_x), rim_of(dy, ext_y)],
            send_sem=send_sem.at[k],
            recv_sem=recv_sem.at[k],
            device_id=peer,
            device_id_type=MESH,
        )
        result.append((exists, send, arrival))
    return result


def start_all(copies):
    for k in (0, 1, 2, 5, 6, 7, 3, 4):
        exists, send, _ = copies[k]
        pl.when(exists)(send.start)


def finish(copies, which):
    for k in which:
        exists, _, arrival = copies[k]
        pl.when(exists)(arrival.wait)


BESIDE, BEYOND = (3, 4), (0, 1, 2, 5, 6, 7)


def fold8(rows):
    return jnp.sum(rows.reshape(rows.shape[0] // 8, 8, rows.shape[1]), axis=0)


def spread_copies(own, slots, send_sem, recv_sem, nodes):
    me, dp = lax.axis_index("space"), lax.axis_index("dp")
    return [
        pltpu.make_async_remote_copy(
            src_ref=own,
            dst_ref=slots.at[step],
            send_sem=send_sem.at[step],
            recv_sem=recv_sem.at[step],
            device_id=(dp, lax.rem(me + step, nodes)),
            device_id_type=MESH,
        )
        for step in range(1, nodes)
    ]


def fill_grid(grid, padded, plane):
    ext_z = padded.shape[2]
    side = jnp.zeros((grid.shape[1], 8, grid.shape[3]), jnp.float32)
    grid[plane, :, pl.ds(0, 8)] = side
    grid[plane, :, pl.ds(8 + ext_z, 8)] = side
    grid[plane, :, pl.ds(8, ext_z)] = padded[plane].astype(jnp.float32)


CHUNKS = 3
LANE = 128


class Summing:
    def __init__(self, nodes, groups, src, out, bufs, sems):
        self.src, self.out = src, out
        self.got_1, self.got_2, self.got_3, self.part_1, self.part_2 = bufs
        self.core_send, self.core_recv, self.plane_send, self.plane_recv, self.line_send, self.line_recv = sems
        self.width = nodes // 4
        self.plane = groups // 2 * self.width
        self.me, self.dp = lax.axis_index("space"), lax.axis_index("dp")
        self.core = lax.rem(self.dp, 2)
        self.line = self.me // self.width
        self.q = (self.dp // 2) * self.width + lax.rem(self.me, self.width)
        self.mate = (self.dp + 1 - 2 * self.core, self.me)
        self.piece = src.shape[0] // (CHUNKS * 2 * self.plane * 4)
        self.made, self.sent = {}, []

    def in_plane(self, step):
        at = lax.rem(self.q + step, self.plane)
        return at, (
            (at // self.width) * 2 + self.core,
            self.line * self.width + lax.rem(at, self.width),
        )

    def in_line(self, step):
        at = lax.rem(self.line + step, 4)
        return at, (self.dp, at * self.width + lax.rem(self.me, self.width))

    def rows(self, c, h, q=None, line=None):
        count = self.piece
        at = (c * 2 + h) * self.plane
        if q is None:
            at, count = at * 4, count * self.plane * 4
        elif line is None:
            at, count = (at + q) * 4, count * 4
        else:
            at = (at + q) * 4 + line
        return pl.ds(pl.multiple_of(at * self.piece, 16), count)

    def copy(self, source, dest, send_sem, recv_sem, peer):
        return pltpu.make_async_remote_copy(
            src_ref=source, dst_ref=dest, send_sem=send_sem, recv_sem=recv_sem,
            device_id=peer, device_id_type=MESH,
        )

    def push(self, key, *args):
        made = self.copy(*args)
        made.start()
        self.made.setdefault(key, []).append(made)

    def give(self, dest, *args):
        made = self.copy(dest, dest, *args)
        made.start()
        self.sent.append(made)

    def taken(self, dest, *args):
        self.copy(dest, dest, *args).wait_recv()

    def finished(self, key):
        for made in self.made[key]:
            made.wait()

    def step_1(self, c):
        self.push((1, c), self.src.at[self.rows(c, 1 - self.core)], self.got_1.at[c],
                  self.core_send.at[0, c], self.core_recv.at[0, c], self.mate)

    def step_2(self, c):
        self.finished((1, c))
        own = self.src[self.rows(c, self.core), :].astype(jnp.float32)
        self.part_1[c] = (own + self.got_1[c].astype(jnp.float32)).astype(jnp.bfloat16)
        count = 4 * self.piece
        for s in range(1, self.plane):
            at, peer = self.in_plane(s)
            self.push((2, c), self.part_1.at[c, pl.ds(pl.multiple_of(at * count, 16), count)],
                      self.got_2.at[c, s], self.plane_send.at[0, c, s],
                      self.plane_recv.at[0, c, s], peer)

    def step_3(self, c):
        self.finished((2, c))
        count = 4 * self.piece
        total = self.part_1[c, pl.ds(pl.multiple_of(self.q * count, 16), count), :].astype(jnp.float32)
        for s in range(1, self.plane):
            total = total + self.got_2[c, s].astype(jnp.float32)
        self.part_2[c] = total.astype(jnp.bfloat16)
        for s in range(1, 4):
            at, peer = self.in_line(s)
            self.push((3, c),
                      self.part_2.at[c, pl.ds(pl.multiple_of(at * self.piece, 16), self.piece)],
                      self.got_3.at[c, s], self.line_send.at[0, c, s],
                      self.line_recv.at[0, c, s], peer)

    def step_4(self, c):
        self.finished((3, c))
        total = self.part_2[
            c, pl.ds(pl.multiple_of(self.line * self.piece, 16), self.piece), :
        ].astype(jnp.float32)
        for s in range(1, 4):
            total = total + self.got_3[c, s].astype(jnp.float32)
        mine = self.rows(c, self.core, self.q, self.line)
        self.out[mine, :] = total.astype(jnp.bfloat16)
        for s in range(1, 4):
            self.give(self.out.at[mine], self.line_send.at[1, c, s], self.line_recv.at[1, c, s],
                      self.in_line(s)[1])

    def step_5(self, c):
        for s in range(1, 4):
            at, peer = self.in_line(4 - s)
            self.taken(self.out.at[self.rows(c, self.core, self.q, at)],
                       self.line_send.at[1, c, s], self.line_recv.at[1, c, s], peer)
        for s in range(1, self.plane):
            self.give(self.out.at[self.rows(c, self.core, self.q)], self.plane_send.at[1, c, s],
                      self.plane_recv.at[1, c, s], self.in_plane(s)[1])

    def step_6(self, c):
        for s in range(1, self.plane):
            at, peer = self.in_plane(self.plane - s)
            self.taken(self.out.at[self.rows(c, self.core, at)],
                       self.plane_send.at[1, c, s], self.plane_recv.at[1, c, s], peer)
        self.give(self.out.at[self.rows(c, self.core)], self.core_send.at[1, c],
                  self.core_recv.at[1, c], self.mate)

    def step_7(self, c):
        self.taken(self.out.at[self.rows(c, 1 - self.core)], self.core_send.at[1, c],
                   self.core_recv.at[1, c], self.mate)

    def close(self):
        for made in self.sent:
            made.wait_send()


def greet(nodes, groups):
    me, dp = lax.axis_index("space"), lax.axis_index("dp")
    width, core = nodes // 4, lax.rem(dp, 2)
    peers = [(dp, lax.rem(me + step, nodes)) for step in range(1, nodes)]
    peers.append((dp + 1 - 2 * core, me))
    for step in range(1, groups // 2):
        other = lax.rem(dp // 2 + step, groups // 2) * 2 + core
        for w in range(width):
            peers.append((other, (me // width) * width + w))
    barrier = pltpu.get_barrier_semaphore()
    for peer in peers:
        pl.semaphore_signal(barrier, inc=1, device_id=peer, device_id_type=MESH)
    pl.semaphore_wait(barrier, len(peers))


GROUP = 4


def level_kernel(
    nodes, groups, fine, w_fine, w_down, depth_w, gain_ref, point_w, up,
    out, out_fine, out_down, out_depth, out_gain, out_point,
    f_pad, stack, pre, act, blocks, g_blocks, g_pre_t,
    coarse, c_pad, g_pad, g_own, g_coarse, c_grid, g_grid, depth_out, g_act, small,
    own_1, own_2, slots_1, slots_2, flat, summed,
    got_1, got_2, got_3, part_1, part_2,
    sem_i, sem_j, sem_a, sem_b, sem_c, sem_d, sem_e, sem_f, sem_g, sem_h,
    *sum_sems,
):
    f32, bf16 = jnp.float32, jnp.bfloat16
    fine_x, fine_y, fine_z, chan = fine.shape
    ext_x, ext_y, ext_z, chans = coarse.shape
    cells = ext_x * ext_y * ext_z
    count = nodes * cells
    f_pad[...] = jnp.zeros_like(f_pad)
    c_pad[...] = jnp.zeros_like(c_pad)
    g_pad[...] = jnp.zeros_like(g_pad)
    greet(nodes, groups)
    total_of = Summing(nodes, groups, flat, summed, (got_1, got_2, got_3, part_1, part_2), sum_sems)
    halo = halo_copies(fine, f_pad, sem_i, sem_j, nodes)
    start_all(halo)
    f_pad[pl.ds(1, fine_x), pl.ds(1, fine_y)] = fine[...]

    def stack_planes(planes):
        spot = lax.broadcasted_iota(jnp.int32, (fine_z, chan), 0)

        def stack_row(y, carry):
            for p in planes:
                row = f_pad[p, y]
                wide = row.astype(f32)
                before = jnp.where(spot == 0, 0.0, pltpu.roll(wide, 1, 0))
                after = jnp.where(spot == fine_z - 1, 0.0, pltpu.roll(wide, fine_z - 1, 0))
                stack[p, y, :, pl.ds(0, chan)] = before.astype(bf16)
                stack[p, y, :, pl.ds(chan, chan)] = row
                stack[p, y, :, pl.ds(2 * chan, chan)] = after.astype(bf16)
            return carry

        lax.fori_loop(0, fine_y + 2, stack_row, 0)

    def conv_planes(planes, first):
        size = GROUP * fine_z

        def conv_group(y_group, carry):
            for x in range(fine_x):
                total = None
                for a in range(3):
                    if x + a not in planes:
                        continue
                    for b in range(3):
                        rows = stack[x + a, pl.ds(y_group * GROUP + b, GROUP)].reshape(size, 3 * chan)
                        term = jnp.dot(
                            rows,
                            w_fine[pl.ds((3 * a + b) * 3 * chan, 3 * chan), :],
                            preferred_element_type=f32,
                        )
                        total = term if total is None else total + term
                at = pl.ds(pl.multiple_of(x * fine_y * fine_z + y_group * size, size), size)
                if total is not None:
                    pre[at, :] = total if first else pre[at, :] + total
            return carry

        lax.fori_loop(0, fine_y // GROUP, conv_group, 0)

    inner, outer = list(range(1, fine_x + 1)), [0, fine_x + 1]
    finish(halo, BESIDE)
    stack_planes(inner)
    conv_planes(inner, True)
    finish(halo, BEYOND)
    stack_planes(outer)
    conv_planes(outer, False)

    def fine_rows(x, y):
        return (x * fine_y + y) * fine_z

    def activate(y, carry):
        for x in range(fine_x):
            at = pl.ds(pl.multiple_of(fine_rows(x, 2 * y), 2 * fine_z), 2 * fine_z)
            value = pre[at, :]
            act[at, :] = (value * jax.nn.sigmoid(value)).astype(bf16).astype(f32)
            for j in range(2):
                for k in range(2):
                    off = 4 * (x % 2) + 2 * j + k
                    part = act[pl.ds(fine_rows(x, 2 * y + j) + k, ext_z, stride=2), :]
                    rows = pl.ds(pl.multiple_of((x // 2 * ext_y + y) * ext_z, ext_z), ext_z)
                    blocks[rows, pl.ds(off * chan, chan)] = part.astype(bf16)
        return carry

    lax.fori_loop(0, ext_y, activate, 0)
    coarse[...] = (
        jnp.dot(blocks[...], w_down[...], preferred_element_type=f32)
        .astype(bf16)
        .reshape(coarse.shape)
    )
    first = halo_copies(coarse, c_pad, sem_a, sem_b, nodes)
    start_all(first)
    c_pad[pl.ds(1, ext_x), pl.ds(1, ext_y)] = coarse[...]
    up_rows = up[...].reshape(cells, chans)
    g_act[...] = lax.dot_general(
        up_rows, point_w[...], (((1,), (1,)), ((), ())), preferred_element_type=f32
    )

    def conv_row(grid, x, y, flip, planes):
        total = None
        for t in range(27):
            a, b, c = tap_offsets(t)
            if x + a not in planes:
                continue
            w_at = 26 - t if flip else t
            term = grid[x + a, y + b, pl.ds(7 + c, ext_z), :] * depth_w[pl.ds(w_at, 1), :]
            total = term if total is None else total + term
        return total

    def cell_rows(x, y):
        return pl.ds(pl.multiple_of((x * ext_y + y) * ext_z, ext_z), ext_z)

    middle, ends = list(range(1, ext_x + 1)), [0, ext_x + 1]
    finish(first, BESIDE)
    for p in middle:
        fill_grid(c_grid, c_pad, p)

    def forward_own(y, carry):
        for x in range(ext_x):
            depth_out[cell_rows(x, y), :] = conv_row(c_grid, x, y, False, middle)
        return carry

    lax.fori_loop(0, ext_y, forward_own, 0)

    def slopes(y, carry):
        for x in range(fine_x):
            at = pl.ds(pl.multiple_of(fine_rows(x, 2 * y), 2 * fine_z), 2 * fine_z)
            value = pre[at, :]
            sigma = jax.nn.sigmoid(value)
            pre[at, :] = sigma * (1.0 + value * (1.0 - sigma))
        return carry

    lax.fori_loop(0, ext_y, slopes, 0)
    finish(first, BEYOND)
    for p in ends:
        fill_grid(c_grid, c_pad, p)

    def forward(y, acc):
        for x in range(ext_x):
            row = depth_out[cell_rows(x, y), :]
            rest = conv_row(c_grid, x, y, False, ends)
            row = row if rest is None else row + rest
            depth_out[cell_rows(x, y), :] = row
            acc = acc + fold8(row * row)
        return acc

    own_1[...] = lax.fori_loop(0, ext_y, forward, jnp.zeros((8, chans), f32))
    spread_1 = spread_copies(own_1, slots_1, sem_c, sem_d, nodes)
    for copy in spread_1:
        copy.start()
    for copy in spread_1:
        copy.wait()
    total = own_1[...]
    for step in range(1, nodes):
        total = total + slots_1[step]
    square_sum = jnp.sum(total, axis=0, keepdims=True)
    gain = gain_ref[...]
    scale = lax.rsqrt(square_sum / count + eps)
    depth_all = depth_out[...]
    normed = (depth_all * (gain * scale)).astype(bf16).astype(f32)
    sigma = jax.nn.sigmoid(normed)
    activated = (normed * sigma).astype(bf16)
    slope = sigma * (1.0 + normed * (1.0 - sigma))
    g_normed = (g_act[...] * slope).astype(bf16).astype(f32)
    g_act[...] = g_normed
    own_2[...] = fold8(g_normed * depth_all)
    spread_2 = spread_copies(own_2, slots_2, sem_e, sem_f, nodes)
    for copy in spread_2:
        copy.start()
    mixed = coarse[...].reshape(cells, chans).astype(f32) + jnp.dot(
        activated, point_w[...], preferred_element_type=f32
    )
    out[...] = mixed.astype(bf16).reshape(coarse.shape)
    down_rows, point_rows = 8 * chan, chans
    at_point, at_small = 2 * down_rows, 2 * down_rows + 2 * point_rows
    at_fine = at_small + 64
    in_point = lax.dot_general(
        activated, up_rows, (((0,), (0,)), ((), ())), preferred_element_type=f32
    ).astype(bf16)
    flat[pl.ds(at_point, point_rows), :] = in_point[:, :LANE]
    flat[pl.ds(at_point + point_rows, point_rows), :] = in_point[:, LANE:]
    small[...] = jnp.zeros_like(small)
    small[pl.ds(27, 1), :] = scale * jnp.sum(own_2[...], axis=0, keepdims=True)
    for copy in spread_2:
        copy.wait()
    total = own_2[...]
    for step in range(1, nodes):
        total = total + slots_2[step]
    cross = jnp.sum(total, axis=0, keepdims=True)
    g_in = gain * scale * g_act[...] - depth_out[...] * (
        gain * scale * scale * scale / count
    ) * cross
    g_own[...] = g_in.astype(bf16).reshape(coarse.shape)
    second = halo_copies(g_own, g_pad, sem_g, sem_h, nodes)
    start_all(second)
    g_pad[pl.ds(1, ext_x), pl.ds(1, ext_y)] = g_own[...]
    for a in range(3):
        def taps(y, acc):
            for x in range(ext_x):
                g_row = g_own[x, y].astype(f32)
                acc = tuple(
                    acc[3 * b + c] + fold8(c_grid[x + a, y + b, pl.ds(7 + c, ext_z), :] * g_row)
                    for b in range(3)
                    for c in range(3)
                )
            return acc
        sums = tuple(jnp.zeros((8, chans), f32) for _ in range(9))
        sums = lax.fori_loop(0, ext_y, taps, sums)
        for k in range(9):
            small[pl.ds(9 * a + k, 1), :] = jnp.sum(sums[k], axis=0, keepdims=True)
    small_16 = small[...].astype(bf16)
    flat[pl.ds(at_small, 32), :] = small_16[:, :LANE]
    flat[pl.ds(at_small + 32, 32), :] = small_16[:, LANE:]
    finish(second, BESIDE + BEYOND)
    for p in middle + ends:
        fill_grid(g_grid, g_pad, p)

    def backward(y, carry):
        for x in range(ext_x):
            row = conv_row(g_grid, x, y, True, middle + ends).astype(bf16).astype(f32)
            g_coarse[cell_rows(x, y), :] = (up[x, y].astype(f32) + row).astype(bf16)
        return carry

    lax.fori_loop(0, ext_y, backward, 0)
    in_down = lax.dot_general(
        blocks[...], g_coarse[...], (((0,), (0,)), ((), ())), preferred_element_type=f32
    ).astype(bf16)
    flat[pl.ds(0, down_rows), :] = in_down[:, :LANE]
    flat[pl.ds(down_rows, down_rows), :] = in_down[:, LANE:]
    total_of.step_1(0)
    g_blocks[...] = lax.dot_general(
        g_coarse[...], w_down[...], (((1,), (1,)), ((), ())), preferred_element_type=f32
    )

    def spread_back(y, carry):
        for x in range(fine_x):
            for j in range(2):
                for k in range(2):
                    off = 4 * (x % 2) + 2 * j + k
                    part = g_blocks[cell_rows(x // 2, y), pl.ds(off * chan, chan)]
                    act[pl.ds(fine_rows(x, 2 * y + j) + k, ext_z, stride=2), :] = part
            start = pl.multiple_of(fine_rows(x, 2 * y), 2 * fine_z)
            at = pl.ds(start, 2 * fine_z)
            g_pre_t[:, at] = (act[at, :] * pre[at, :]).T.astype(bf16)
        return carry

    lax.fori_loop(0, ext_y, spread_back, 0)

    def weight_grads(low, high):
        def one(at, carry):
            rows = stack[pl.ds(at // 3, fine_x), pl.ds(lax.rem(at, 3), fine_y)]
            turned = jnp.dot(
                g_pre_t[...],
                rows.reshape(fine_x * fine_y * fine_z, 3 * chan),
                preferred_element_type=f32,
            )
            for c in range(3):
                start = pl.multiple_of(at_fine + (3 * at + c) * chan, 16)
                flat[pl.ds(start, chan), :] = turned[:, c * chan : (c + 1) * chan].T.astype(bf16)
            return carry

        lax.fori_loop(low, high, one, 0)

    used = at_fine + 27 * chan
    if used < flat.shape[0]:
        flat[pl.ds(used, flat.shape[0] - used), :] = jnp.zeros(
            (flat.shape[0] - used, LANE), bf16
        )
    split = min(9, -(-(2 * (flat.shape[0] // CHUNKS) - at_fine) // (3 * chan)))
    weight_grads(0, split)
    total_of.step_1(1)
    total_of.step_2(0)
    weight_grads(split, 9)
    total_of.step_1(2)
    for c in range(1, CHUNKS):
        total_of.step_2(c)
        total_of.step_3(c - 1)
    total_of.step_4(0)
    total_of.step_3(CHUNKS - 1)
    total_of.step_5(0)
    for c in range(1, CHUNKS):
        total_of.step_4(c)
    for c in range(1, CHUNKS):
        total_of.step_5(c)
    for c in range(CHUNKS):
        total_of.step_6(c)
    total_of.step_7(0)
    out_down[:, pl.ds(0, LANE)] = summed[pl.ds(0, down_rows), :].astype(f32)
    out_down[:, pl.ds(LANE, LANE)] = summed[pl.ds(down_rows, down_rows), :].astype(f32)
    for c in range(1, CHUNKS):
        total_of.step_7(c)
    for part in range(2):
        lanes = pl.ds(part * LANE, LANE)
        out_point[:, lanes] = summed[
            pl.ds(at_point + part * point_rows, point_rows), :
        ].astype(f32)
        small[:, lanes] = summed[pl.ds(at_small + 32 * part, 32), :].astype(f32)
    out_depth[...] = small[pl.ds(0, 27), :]
    out_gain[...] = small[pl.ds(27, 1), :]
    out_fine[...] = summed[pl.ds(at_fine, 27 * chan), :].astype(f32)
    total_of.close()


def whole_level(fine, w_fine, w_down, depth_w, gain, point_w, up, nodes, groups):
    f32, bf16, dma = jnp.float32, jnp.bfloat16, pltpu.SemaphoreType.DMA
    fine_x, fine_y, fine_z, chan = fine.shape
    ext_x, ext_y, ext_z, chans = up.shape
    cells, fine_cells = ext_x * ext_y * ext_z, fine_x * fine_y * fine_z
    padded = (ext_x + 2, ext_y + 2, ext_z, chans)
    grid = (ext_x + 2, ext_y + 2, ext_z + 16, chans)
    plane = groups // 2 * (nodes // 4)
    unit = CHUNKS * 2 * plane * 4 * 16
    rows = 16 * chan + 2 * chans + 64 + 27 * chan
    rows = -(-rows // unit) * unit
    piece = rows // (CHUNKS * 2 * plane * 4)
    return pl.pallas_call(
        functools.partial(level_kernel, nodes, groups),
        out_shape=(
            jax.ShapeDtypeStruct(up.shape, bf16),
            jax.ShapeDtypeStruct((27 * chan, chan), f32),
            jax.ShapeDtypeStruct((8 * chan, chans), f32),
            jax.ShapeDtypeStruct((27, chans), f32),
            jax.ShapeDtypeStruct((1, chans), f32),
            jax.ShapeDtypeStruct((chans, chans), f32),
        ),
        in_specs=[VMEM_SPEC] * 7,
        out_specs=(VMEM_SPEC,) * 6,
        scratch_shapes=[
            pltpu.VMEM((fine_x + 2, fine_y + 2, fine_z, chan), bf16),
            pltpu.VMEM((fine_x + 2, fine_y + 2, fine_z, 3 * chan), bf16),
            pltpu.VMEM((fine_cells, chan), f32),
            pltpu.VMEM((fine_cells, chan), f32),
            pltpu.VMEM((cells, 8 * chan), bf16),
            pltpu.VMEM((cells, 8 * chan), f32),
            pltpu.VMEM((chan, fine_cells), bf16),
            pltpu.VMEM(up.shape, bf16),
            pltpu.VMEM(padded, bf16),
            pltpu.VMEM(padded, bf16),
            pltpu.VMEM(up.shape, bf16),
            pltpu.VMEM((cells, chans), bf16),
            pltpu.VMEM(grid, f32),
            pltpu.VMEM(grid, f32),
            pltpu.VMEM((cells, chans), f32),
            pltpu.VMEM((cells, chans), f32),
            pltpu.VMEM((32, chans), f32),
            pltpu.VMEM((8, chans), f32),
            pltpu.VMEM((8, chans), f32),
            pltpu.VMEM((nodes, 8, chans), f32),
            pltpu.VMEM((nodes, 8, chans), f32),
            pltpu.VMEM((rows, LANE), bf16),
            pltpu.VMEM((rows, LANE), bf16),
            pltpu.VMEM((CHUNKS, plane * 4 * piece, LANE), bf16),
            pltpu.VMEM((CHUNKS, plane, 4 * piece, LANE), bf16),
            pltpu.VMEM((CHUNKS, 4, piece, LANE), bf16),
            pltpu.VMEM((CHUNKS, plane * 4 * piece, LANE), bf16),
            pltpu.VMEM((CHUNKS, 4 * piece, LANE), bf16),
            dma((8,)), dma((8,)),
            dma((8,)), dma((8,)), dma((nodes,)), dma((nodes,)),
            dma((nodes,)), dma((nodes,)), dma((8,)), dma((8,)),
            dma((2, CHUNKS)), dma((2, CHUNKS)),
            dma((2, CHUNKS, plane)), dma((2, CHUNKS, plane)),
            dma((2, CHUNKS, 4)), dma((2, CHUNKS, 4)),
        ],
        compiler_params=pltpu.CompilerParams(
            collective_id=0, has_side_effects=True, vmem_limit_bytes=VMEM_BYTES
        ),
        name="whole_level",
    )(fine, w_fine.reshape(-1, w_fine.shape[2]), w_down, depth_w, gain.reshape(1, chans), point_w, up)


def local(fields, conv_fine, conv_down, conv_depth, norm_gain, conv_point, upstream):
    nodes, groups = lax.axis_size("space"), lax.axis_size("dp")
    coarse_out, fine, down, depth, gain, point = whole_level(
        fields[0, 0], conv_fine, conv_down, conv_depth, norm_gain, conv_point, upstream[0, 0],
        nodes, groups,
    )
    return (
        coarse_out[None, None], fine.reshape(conv_fine.shape), down, depth, gain.reshape(-1), point
    )


def solution(mesh):
    placed = (
        P("dp", "space", None, None, None, None),
        P(),
        P(),
        P(),
        P(),
        P(),
        P("dp", "space", None, None, None, None),
    )
    return jax.shard_map(
        local,
        mesh=mesh,
        in_specs=placed,
        out_specs=(P("dp", "space", None, None, None, None), P(), P(), P(), P(), P()),
        check_vma=False,
    )
```

time: 136 us -> 90.1 us (0.66)
  matrix products: 21.1 us -> 0 us
  local copies, waits for them, and re-layouts: 28.7 us -> 11.2 us
  other arithmetic: 4.49 us -> 0 us
  Pallas kernels: 79.3 us -> 77.8 us
    dot_general x57 -> x0, matrix products: 21.1 us -> none  [the longest x27 9.68 us: tap_grads(): lax.dot_general(window, grad_rows, (((0,), (0,)), ((), ())), preferred_el...]
    reshape x7 -> x0, local copies, waits for them, and re-layouts: 7.03 us -> none  [the longest x3 2.66 us: sum_everywhere(): result.append(summed[at:at + count].astype(jnp.float32).reshape(grad.shape))]
    slice x4 -> x0, local copies, waits for them, and re-layouts: 5.36 us -> none  [the longest x3 4.13 us: full_conv(): padded[shift_x:shift_x + ext_x, shift_y:shift_y + ext_y, shift_z:shift_z...]
    reshape x5 -> x0, other arithmetic: 4.06 us -> none  [sum_everywhere(): result.append(summed[at:at + count].astype(jnp.float32).reshape(grad.shape))]
    concatenate x1 -> x0, local copies, waits for them, and re-layouts: 4.02 us -> none  [sum_everywhere(): jnp.concatenate(flat, axis=0).reshape(CHUNKS, 2, plane, 4, piece, lane)]
    pallas_call x3 -> x1, Pallas kernels: 79.3 us -> 77.8 us  [whole_level(): pl.pallas_call(functools.partial(level_kernel, nodes, groups), out_shape=...]
    unnamed x121 -> x20, local copies, waits for them, and re-layouts: 10.3 us -> 11.2 us
where the time goes in v2:
time: 90.1 us; the launch traced here: 89.7 us
  Pallas kernels  77.8 us (86%)
  local copies, waits for them, and re-layouts  11.2 us (12%)
    pallas_call x1, Pallas kernels, whole_level(): pl.pallas_call(functools.partial(level_kernel, nodes, groups), out_shape=...  77.8 us
    unnamed x20, local copies, waits for them, and re-layouts  11.2 us

profile of v2, /device:TPU:0, one launch (start us, length us, event | category | flops | bytes accessed | tf_op | source)
XLA Modules:
  0.0 89.7 jit_solution(4236722241874874783)
XLA Ops:
  0.6 0.0 copy-start
  0.6 1.2 %copy-done = bf16[27,128,128]{2,1,0:T(8,128)(2,1)S(1)} copy-done((bf16[27,128,128]{2,1,0:T(8,128)(2,1)S(1)}, bf16[27,128,128]{2,1,0:T(8,128)(2,1)}, u32[]{:S(2)}) %copy-start) | copy-done | bytes 884760
  1.8 0.0 copy-start.1
  1.8 1.0 %copy-done.1 = bf16[1,1,2,16,64,128]{5,4,3,2,1,0:T(8,128)(2,1)S(1)} copy-done((bf16[1,1,2,16,64,128]{5,4,3,2,1,0:T(8,128)(2,1)S(1)}, bf16[1,1,2,16,64,128]{5,4,3,2,1,0:T(8,128)(2,1)}, u32[]{:S(2)}) %copy-start.1) | copy-done | bytes 524312
  2.8 0.0 copy-start.2
  2.8 1.0 %copy-done.2 = bf16[1024,256]{1,0:T(8,128)(2,1)S(1)} copy-done((bf16[1024,256]{1,0:T(8,128)(2,1)S(1)}, bf16[1024,256]{1,0:T(8,128)(2,1)}, u32[]{:S(2)}) %copy-start.2) | copy-done | bytes 524312
  3.9 0.0 copy-start.3
  3.9 0.9 %copy-done.3 = bf16[256,256]{1,0:T(8,128)(2,1)S(1)} copy-done((bf16[256,256]{1,0:T(8,128)(2,1)S(1)}, bf16[256,256]{1,0:T(8,128)(2,1)}, u32[]{:S(2)}) %copy-start.3) | copy-done | bytes 131096
  4.8 0.0 copy-start.4
  4.8 0.9 %copy-done.4 = bf16[1,1,1,8,32,256]{5,4,3,2,1,0:T(8,128)(2,1)S(1)} copy-done((bf16[1,1,1,8,32,256]{5,4,3,2,1,0:T(8,128)(2,1)S(1)}, bf16[1,1,1,8,32,256]{5,4,3,2,1,0:T(8,128)(2,1)}, u32[]{:S(2)}) %copy-start.4) | copy-done | bytes 131096
  5.7 0.0 copy-start.5
  5.7 0.8 copy-done.5
  6.5 0.0 copy-start.6
  6.5 0.7 copy-done.6
  7.1 77.8 %whole_level.1 = (bf16[1,8,32,256]{3,2,1,0:T(8,128)(2,1)S(1)}, f32[3456,128]{1,0:T(8,128)S(1)}, f32[1024,256]{1,0:T(8,128)S(1)}, f32[27,256]{1,0:T(8,128)S(1)}, ...) custom-call(bf16[2,16,64,128]{3,2,1,0:T(8,128)(2,1)S(1)} %bitcast.9, bf16[3456,128]{1,0:T(8,128)(2,1)S(1)} %bitcast.8, ...), custom_call_target="tpu_custom_call" | custom-call | tf_op jit(solution)/shard_map/whole_level/pallas_call | solution.py:571
  84.9 0.7 copy.19
  85.6 1.2 %copy.20 = f32[27,128,128]{2,1,0:T(8,128)} copy(f32[27,128,128]{2,1,0:T(8,128)S(1)} %bitcast.7) | data formatting | bytes 3538944
  86.8 1.0 %copy.21 = f32[1024,256]{1,0:T(8,128)} copy(f32[1024,256]{1,0:T(8,128)S(1)} %get-tuple-element.26) | data formatting | bytes 2097152
  87.8 0.6 copy.22
  88.4 0.6 copy.23
  88.9 0.7 copy.24
Async XLA Ops:
  0.6 1.2 %copy-start = (bf16[27,128,128]{2,1,0:T(8,128)(2,1)S(1)}, bf16[27,128,128]{2,1,0:T(8,128)(2,1)}, u32[]{:S(2)}) copy-start(bf16[27,128,128]{2,1,0:T(8,128)(2,1)} %param.8) | copy-start | bytes 2654212
  1.8 1.0 %copy-start.1 = (bf16[1,1,2,16,64,128]{5,4,3,2,1,0:T(8,128)(2,1)S(1)}, bf16[1,1,2,16,64,128]{5,4,3,2,1,0:T(8,128)(2,1)}, u32[]{:S(2)}) copy-start(bf16[1,1,2,16,64,128]{5,4,3,2,1,0:T(8,128)(2,1)} %param.7) | copy-start | bytes 1572868
  2.8 1.0 %copy-start.2 = (bf16[1024,256]{1,0:T(8,128)(2,1)S(1)}, bf16[1024,256]{1,0:T(8,128)(2,1)}, u32[]{:S(2)}) copy-start(bf16[1024,256]{1,0:T(8,128)(2,1)} %w_down.1) | copy-start | bytes 1572868
  3.9 0.9 %copy-start.3 = (bf16[256,256]{1,0:T(8,128)(2,1)S(1)}, bf16[256,256]{1,0:T(8,128)(2,1)}, u32[]{:S(2)}) copy-start(bf16[256,256]{1,0:T(8,128)(2,1)} %point_w.1) | copy-start | bytes 393220
  4.8 0.9 %copy-start.4 = (bf16[1,1,1,8,32,256]{5,4,3,2,1,0:T(8,128)(2,1)S(1)}, bf16[1,1,1,8,32,256]{5,4,3,2,1,0:T(8,128)(2,1)}, u32[]{:S(2)}) copy-start(bf16[1,1,1,8,32,256]{5,4,3,2,1,0:T(8,128)(2,1)} %param.13) | copy-start | bytes 393220
  5.7 0.8 copy-start.5
  6.5 0.7 copy-start.6

commit v3 on v2

--- a/solution.py
+++ b/solution.py
@@ -10,7 +10,8 @@
 MESH = pl.DeviceIdType.MESH
 OFFSETS = [(dx, dy) for dx in (-1, 0, 1) for dy in (-1, 0, 1) if (dx, dy) != (0, 0)]
 VMEM_SPEC = pl.BlockSpec(memory_space=pltpu.VMEM)
-VMEM_BYTES = 48 * 1024 * 1024
+ANY_SPEC = pl.BlockSpec(memory_space=pl.ANY)
+VMEM_BYTES = 61 * 1024 * 1024
 
 
 def tap_offsets(tap_index):
@@ -58,7 +59,7 @@
 
 
 def start_all(copies):
-    for k in (0, 1, 2, 5, 6, 7, 3, 4):
+    for k in (3, 4, 1, 6, 0, 2, 5, 7):
         exists, send, _ = copies[k]
         pl.when(exists)(send.start)
 
@@ -250,11 +251,12 @@
 
 
 def level_kernel(
-    nodes, groups, fine, w_fine, w_down, depth_w, gain_ref, point_w, up,
-    out, out_fine, out_down, out_depth, out_gain, out_point,
+    nodes, groups, fine, w_fine_in, w_down_in, depth_w_in, gain_in, point_w_in, up_in,
+    out, summed,
+    w_fine, w_down, depth_w, gain_ref, point_w, up, sem_in,
     f_pad, stack, pre, act, blocks, g_blocks, g_pre_t,
     coarse, c_pad, g_pad, g_own, g_coarse, c_grid, g_grid, depth_out, g_act, small,
-    own_1, own_2, slots_1, slots_2, flat, summed,
+    own_1, own_2, slots_1, slots_2, flat,
     got_1, got_2, got_3, part_1, part_2,
     sem_i, sem_j, sem_a, sem_b, sem_c, sem_d, sem_e, sem_f, sem_g, sem_h,
     *sum_sems,
@@ -266,12 +268,21 @@
     count = nodes * cells
     f_pad[...] = jnp.zeros_like(f_pad)
     c_pad[...] = jnp.zeros_like(c_pad)
+    loads = [
+        pltpu.make_async_copy(source, dest, sem_in.at[k])
+        for k, (source, dest) in enumerate((
+            (fine, f_pad.at[pl.ds(1, fine_x), pl.ds(1, fine_y)]),
+            (w_fine_in, w_fine), (w_down_in, w_down), (depth_w_in, depth_w),
+            (gain_in, gain_ref), (point_w_in, point_w), (up_in, up),
+        ))
+    ]
+    for load in loads:
+        load.start()
     g_pad[...] = jnp.zeros_like(g_pad)
     greet(nodes, groups)
     total_of = Summing(nodes, groups, flat, summed, (got_1, got_2, got_3, part_1, part_2), sum_sems)
     halo = halo_copies(fine, f_pad, sem_i, sem_j, nodes)
     start_all(halo)
-    f_pad[pl.ds(1, fine_x), pl.ds(1, fine_y)] = fine[...]
 
     def stack_planes(planes):
         spot = lax.broadcasted_iota(jnp.int32, (fine_z, chan), 0)
@@ -314,6 +325,8 @@
         lax.fori_loop(0, fine_y // GROUP, conv_group, 0)
 
     inner, outer = list(range(1, fine_x + 1)), [0, fine_x + 1]
+    for load in loads:
+        load.wait()
     finish(halo, BESIDE)
     stack_planes(inner)
     conv_planes(inner, True)
@@ -539,21 +552,46 @@
         total_of.step_5(c)
     for c in range(CHUNKS):
         total_of.step_6(c)
-    total_of.step_7(0)
-    out_down[:, pl.ds(0, LANE)] = summed[pl.ds(0, down_rows), :].astype(f32)
-    out_down[:, pl.ds(LANE, LANE)] = summed[pl.ds(down_rows, down_rows), :].astype(f32)
-    for c in range(1, CHUNKS):
+    for c in range(CHUNKS):
         total_of.step_7(c)
+    total_of.close()
+
+
+def unpack_kernel(
+    summed, coarse_in, out, out_fine, out_down, out_depth, out_gain, out_point,
+    fine, down, depth, gain, point, sems,
+):
+    f32 = jnp.float32
+    down_rows, point_rows = down.shape[0], point.shape[0]
+    at_point, at_small = 2 * down_rows, 2 * down_rows + 2 * point_rows
+    at_fine = at_small + 64
+    sent = []
+
+    def send(source, dest):
+        copy = pltpu.make_async_copy(source, dest, sems.at[len(sent)])
+        copy.start()
+        sent.append(copy)
+
+    send(coarse_in, out)
+    fine[...] = summed[pl.ds(at_fine, fine.shape[0]), :].astype(f32)
+    send(fine, out_fine)
     for part in range(2):
         lanes = pl.ds(part * LANE, LANE)
-        out_point[:, lanes] = summed[
+        down[:, lanes] = summed[pl.ds(part * down_rows, down_rows), :].astype(f32)
+    send(down, out_down)
+    for part in range(2):
+        lanes = pl.ds(part * LANE, LANE)
+        point[:, lanes] = summed[
             pl.ds(at_point + part * point_rows, point_rows), :
         ].astype(f32)
-        small[:, lanes] = summed[pl.ds(at_small + 32 * part, 32), :].astype(f32)
-    out_depth[...] = small[pl.ds(0, 27), :]
-    out_gain[...] = small[pl.ds(27, 1), :]
-    out_fine[...] = summed[pl.ds(at_fine, 27 * chan), :].astype(f32)
-    total_of.close()
+        small = summed[pl.ds(at_small + 32 * part, 32), :].astype(f32)
+        depth[:, lanes] = small[:27]
+        gain[:, lanes] = small[27:28]
+    send(point, out_point)
+    send(depth, out_depth)
+    send(gain, out_gain)
+    for copy in sent:
+        copy.wait()
 
 
 def whole_level(fine, w_fine, w_down, depth_w, gain, point_w, up, nodes, groups):
@@ -568,19 +606,30 @@
     rows = 16 * chan + 2 * chans + 64 + 27 * chan
     rows = -(-rows // unit) * unit
     piece = rows // (CHUNKS * 2 * plane * 4)
-    return pl.pallas_call(
-        functools.partial(level_kernel, nodes, groups),
-        out_shape=(
+    results = (
             jax.ShapeDtypeStruct(up.shape, bf16),
             jax.ShapeDtypeStruct((27 * chan, chan), f32),
             jax.ShapeDtypeStruct((8 * chan, chans), f32),
             jax.ShapeDtypeStruct((27, chans), f32),
             jax.ShapeDtypeStruct((1, chans), f32),
             jax.ShapeDtypeStruct((chans, chans), f32),
+    )
+    coarse_out, summed = pl.pallas_call(
+        functools.partial(level_kernel, nodes, groups),
+        out_shape=(
+            jax.ShapeDtypeStruct(up.shape, bf16),
+            jax.ShapeDtypeStruct((rows, LANE), bf16),
         ),
-        in_specs=[VMEM_SPEC] * 7,
-        out_specs=(VMEM_SPEC,) * 6,
+        in_specs=[ANY_SPEC] * 7,
+        out_specs=(VMEM_SPEC,) * 2,
         scratch_shapes=[
+            pltpu.VMEM((27 * chan, chan), bf16),
+            pltpu.VMEM(w_down.shape, bf16),
+            pltpu.VMEM(depth_w.shape, f32),
+            pltpu.VMEM((1, chans), f32),
+            pltpu.VMEM(point_w.shape, bf16),
+            pltpu.VMEM(up.shape, bf16),
+            dma((7,)),
             pltpu.VMEM((fine_x + 2, fine_y + 2, fine_z, chan), bf16),
             pltpu.VMEM((fine_x + 2, fine_y + 2, fine_z, 3 * chan), bf16),
             pltpu.VMEM((fine_cells, chan), f32),
@@ -603,7 +652,6 @@
             pltpu.VMEM((nodes, 8, chans), f32),
             pltpu.VMEM((nodes, 8, chans), f32),
             pltpu.VMEM((rows, LANE), bf16),
-            pltpu.VMEM((rows, LANE), bf16),
             pltpu.VMEM((CHUNKS, plane * 4 * piece, LANE), bf16),
             pltpu.VMEM((CHUNKS, plane, 4 * piece, LANE), bf16),
             pltpu.VMEM((CHUNKS, 4, piece, LANE), bf16),
@@ -621,6 +669,15 @@
         ),
         name="whole_level",
     )(fine, w_fine.reshape(-1, w_fine.shape[2]), w_down, depth_w, gain.reshape(1, chans), point_w, up)
+    return pl.pallas_call(
+        unpack_kernel,
+        out_shape=results,
+        in_specs=[VMEM_SPEC] * 2,
+        out_specs=(ANY_SPEC,) * 6,
+        scratch_shapes=[pltpu.VMEM(one.shape, one.dtype) for one in results[1:]] + [dma((6,))],
+        compiler_params=pltpu.CompilerParams(vmem_limit_bytes=VMEM_BYTES),
+        name="unpack",
+    )(summed, coarse_out)
 
 
 def local(fields, conv_fine, conv_down, conv_depth, norm_gain, conv_point, upstream):

time: 90.1 us -> 83.6 us (0.928)
  local copies, waits for them, and re-layouts: 11.2 us -> 0 us
  Pallas kernels: 77.8 us -> 82.8 us
    unnamed x20 -> x0, local copies, waits for them, and re-layouts: 11.2 us -> none
    pallas_call x0 -> x1, Pallas kernels: none -> 3.21 us  [whole_level(): pl.pallas_call(unpack_kernel, out_shape=results, in_specs=[VMEM_SPEC] * 2...]
    pallas_call x1, Pallas kernels: 77.8 us -> 79.6 us  [whole_level(): pl.pallas_call(functools.partial(level_kernel, nodes, groups), out_shape=...]
where the time goes in v3:
time: 83.6 us; the launch traced here: 83.5 us
  Pallas kernels  82.8 us (99%)
    pallas_call x1, Pallas kernels, whole_level(): pl.pallas_call(functools.partial(level_kernel, nodes, groups), out_shape=...  79.6 us
    pallas_call x1, Pallas kernels, whole_level(): pl.pallas_call(unpack_kernel, out_shape=results, in_specs=[VMEM_SPEC] * 2...  3.21 us

profile of v3, /device:TPU:0, one launch (start us, length us, event | category | flops | bytes accessed | tf_op | source)
XLA Modules:
  0.0 83.5 jit_solution(11628663116454384819)
XLA Ops:
  0.6 79.6 %whole_level.1 = (bf16[1,8,32,256]{3,2,1,0:T(8,128)(2,1)}, bf16[6144,128]{1,0:T(8,128)(2,1)}) custom-call(bf16[2,16,64,128]{3,2,1,0:T(8,128)(2,1)} %bitcast.8, bf16[3456,128]{1,0:T(8,128)(2,1)} %bitcast.7, bf16[1024,256]{1,0:T(8,128)(2,1)} %w_down_in.1, f32[27,256]{1,0:T(8,128)} %depth_w_in.1, f32[1,256]{1,0:T(1,128)} %bitcast.10, ...), custom_call_target="tpu_custom_call" | custom-call | tf_op jit(solution)/shard_map/whole_level/pallas_call | solution.py:617
  80.3 3.2 %unpack.1 = (bf16[1,8,32,256]{3,2,1,0:T(8,128)(2,1)}, f32[3456,128]{1,0:T(8,128)}, f32[1024,256]{1,0:T(8,128)}, f32[27,256]{1,0:T(8,128)}, f32[1,256]{1,0:T(1,128)}, /*index=5*/f32[256,256]{1,0:T(8,128)}) custom-call(bf16[6144,128]{1,0:T(8,128)(2,1)} %get-tuple-element.14.summed, bf16[1,8,32,256]{3,2,1,0:T(8,128)(2,1)} %get-tuple-element.15.coarse_in), custom_call_target="tpu_custom_call" | custom-call | tf_op jit(solution)/shard_map/unpack/pallas_call | solution.py:672

commit v4 on v3

--- a/solution.py
+++ b/solution.py
@@ -535,23 +535,27 @@
             (flat.shape[0] - used, LANE), bf16
         )
     split = min(9, -(-(2 * (flat.shape[0] // CHUNKS) - at_fine) // (3 * chan)))
+    half = (split + 9) // 2
+    total_of.step_2(0)
     weight_grads(0, split)
     total_of.step_1(1)
-    total_of.step_2(0)
-    weight_grads(split, 9)
+    total_of.step_3(0)
+    weight_grads(split, half)
+    total_of.step_2(1)
+    total_of.step_4(0)
+    weight_grads(half, 9)
     total_of.step_1(2)
-    for c in range(1, CHUNKS):
-        total_of.step_2(c)
-        total_of.step_3(c - 1)
-    total_of.step_4(0)
-    total_of.step_3(CHUNKS - 1)
+    total_of.step_3(1)
     total_of.step_5(0)
-    for c in range(1, CHUNKS):
-        total_of.step_4(c)
-    for c in range(1, CHUNKS):
-        total_of.step_5(c)
-    for c in range(CHUNKS):
-        total_of.step_6(c)
+    total_of.step_2(2)
+    total_of.step_4(1)
+    total_of.step_6(0)
+    total_of.step_3(2)
+    total_of.step_5(1)
+    total_of.step_4(2)
+    total_of.step_6(1)
+    total_of.step_5(2)
+    total_of.step_6(2)
     for c in range(CHUNKS):
         total_of.step_7(c)
     total_of.close()

time: 83.6 us -> 89.4 us (1.069)
  Pallas kernels: 82.8 us -> 88.6 us
    pallas_call x1, Pallas kernels: 79.6 us -> 85.4 us  [whole_level(): pl.pallas_call(functools.partial(level_kernel, nodes, groups), out_shape=...]
where the time goes in v4:
time: 89.4 us; the launch traced here: 89.3 us
  Pallas kernels  88.6 us (99%)
    pallas_call x1, Pallas kernels, whole_level(): pl.pallas_call(functools.partial(level_kernel, nodes, groups), out_shape=...  85.4 us
    pallas_call x1, Pallas kernels, whole_level(): pl.pallas_call(unpack_kernel, out_shape=results, in_specs=[VMEM_SPEC] * 2...  3.21 us

profile of v4, /device:TPU:0, one launch (start us, length us, event | category | flops | bytes accessed | tf_op | source)
XLA Modules:
  0.0 89.3 jit_solution(16955031497490169610)
XLA Ops:
  0.6 85.4 %whole_level.1 = (bf16[1,8,32,256]{3,2,1,0:T(8,128)(2,1)}, bf16[6144,128]{1,0:T(8,128)(2,1)}) custom-call(bf16[2,16,64,128]{3,2,1,0:T(8,128)(2,1)} %bitcast.8, bf16[3456,128]{1,0:T(8,128)(2,1)} %bitcast.7, bf16[1024,256]{1,0:T(8,128)(2,1)} %w_down_in.1, f32[27,256]{1,0:T(8,128)} %depth_w_in.1, f32[1,256]{1,0:T(1,128)} %bitcast.10, ...), custom_call_target="tpu_custom_call" | custom-call | tf_op jit(solution)/shard_map/whole_level/pallas_call | solution.py:621
  86.1 3.2 %unpack.1 = (bf16[1,8,32,256]{3,2,1,0:T(8,128)(2,1)}, f32[3456,128]{1,0:T(8,128)}, f32[1024,256]{1,0:T(8,128)}, f32[27,256]{1,0:T(8,128)}, f32[1,256]{1,0:T(1,128)}, /*index=5*/f32[256,256]{1,0:T(8,128)}) custom-call(bf16[6144,128]{1,0:T(8,128)(2,1)} %get-tuple-element.14.summed, bf16[1,8,32,256]{3,2,1,0:T(8,128)(2,1)} %get-tuple-element.15.coarse_in), custom_call_target="tpu_custom_call" | custom-call | tf_op jit(solution)/shard_map/unpack/pallas_call | solution.py:676
